TPU v7x, 512 devices: a whole 4x4x16 slice. The times are simulated.
512 devices in a mesh: row: 16 (over y, x), col: 32 (over z, core).
Axes of the slice: x: 4, y: 4, z: 16, core: 2. Of those that a mesh axis runs over, the one named last changes fastest.
Arguments:
- points: float32 [8, 65536], P(None, ('row', 'col')), may hold values from -6 to 6
- lengthscale: float32 [8], replicated, may hold values from 1.5 to 4
- signal_var: float32 [1], replicated, may hold values from 0.002 to 0.01
- noise_var: float32 [1], replicated, may hold values from 0.3 to 1.5
- solution: float32 [4, 65536], P(None, ('row', 'col')), may hold values from -6 to 6
- residual: float32 [4, 65536], P(None, ('row', 'col')), may hold values from -30 to 30, as said below
- direction: float32 [4, 65536], P(None, ('row', 'col')), may hold values from -6 to 6
Outputs:
- new_solution: float32 [4, 65536], P(None, ('row', 'col'))
- new_residual: float32 [4, 65536], P(None, ('row', 'col'))
- new_direction: float32 [4, 65536], P(None, ('row', 'col'))
Inputs may be any that keep to these rules, and one draw needn't show every extreme that they name: residual values, real-valued.
All inputs are finite; a program needn't handle non-finite values.
Results may differ from a plain program's by a relative error of at most 0.00017.
Values sent between devices are 32-bit elements; how exact they have to be, the bound alone decides.
No kernel may reach another device: no remote copies, remote signals or barrier semaphores. Data moves between devices by JAX's collectives and lax.ppermute only.
A program may use at most 128 MiB of HBM per device.

v0:
```python
import jax
import jax.numpy as jnp
from jax import lax
from jax.sharding import PartitionSpec as P


def kernel_apply(row_pts, col_pts, col_dir, scale):
    rows = row_pts.shape[1]
    block = min(256, rows)
    blocks = row_pts.reshape(row_pts.shape[0], rows // block, block).transpose(1, 0, 2)

    def one_block(left):
        dist_sq = jnp.zeros((left.shape[1], col_pts.shape[1]), jnp.float32)
        for dim_idx in range(left.shape[0]):
            delta = left[dim_idx][:, None] - col_pts[dim_idx][None, :]
            dist_sq = dist_sq + delta * delta
        radius = jnp.sqrt(dist_sq)
        root_five = jnp.sqrt(jnp.float32(5.0))
        values = (
            scale * (1.0 + root_five * radius + 5.0 / 3.0 * dist_sq) * jnp.exp(-root_five * radius)
        )
        return jnp.einsum("rc,kc->kr", values, col_dir, precision=lax.Precision.HIGHEST)

    result = lax.map(one_block, blocks)
    return result.transpose(1, 0, 2).reshape(col_dir.shape[0], rows)


def on_device(points, lengthscale, signal_var, noise_var, solution, residual, direction):
    scaled = points / lengthscale[:, None]
    all_pts, all_dir = (
        lax.all_gather(scaled, ("row", "col"), axis=1, tiled=True),
        lax.all_gather(direction, ("row", "col"), axis=1, tiled=True),
    )
    applied = kernel_apply(scaled, all_pts, all_dir, signal_var[0])
    image = applied + noise_var[0] * direction
    old_rr = lax.psum(jnp.sum(residual * residual, axis=1), ("row", "col"))
    curv = lax.psum(jnp.sum(direction * image, axis=1), ("row", "col"))
    alpha = old_rr / curv
    new_solution = solution + alpha[:, None] * direction
    new_residual = residual - alpha[:, None] * image
    new_rr = lax.psum(jnp.sum(new_residual * new_residual, axis=1), ("row", "col"))
    new_direction = new_residual + (new_rr / old_rr)[:, None] * direction
    return (new_solution, new_residual, new_direction)


def solution(mesh):
    in_specs = (
        P(None, ("row", "col")),
        P(),
        P(),
        P(),
        P(None, ("row", "col")),
        P(None, ("row", "col")),
        P(None, ("row", "col")),
    )
    out_specs = (P(None, ("row", "col")), P(None, ("row", "col")), P(None, ("row", "col")))
    return jax.shard_map(
        on_device, mesh=mesh, in_specs=in_specs, out_specs=out_specs, check_vma=False
    )
```

profile of v0, /device:TPU:1, one launch (start us, length us, event | category | flops | bytes accessed | tf_op | source)
XLA Modules:
  0.0 618.3 jit_solution(1967070852810441112)
XLA Ops:
  7.2 0.0 copy-start
  7.2 0.0 all-gather.3.cloned.1.call-start
  7.2 1.4 broadcast_divide_fusion
  8.6 0.0 all-gather.3.cloned.1.call-update
  8.6 0.0 all-gather.5.cloned.1.call-start
  8.7 0.7 all-gather.5.cloned.1.call-update
  9.4 1.0 slice_bitcast_fusion.7
  11.6 0.8 multiply_reduce_fusion.2
  12.4 199.5 %all-gather.3.cloned.1.call-done = f32[8,65536]{1,0:T(8,128)} async-done(((f32[8,128]{1,0:T(8,128)}), f32[8,65536]{1,0:T(8,128)}) %all-gather.3.cloned.1.call-update) | async-done | bytes 2097168 | tf_op jit(solution)/shard_map/all_gather | solution.py:31
  212.0 8.6 %fusion.64 = (f32[1,65536]{1,0:T(1,128)S(1)}, f32[1,65536]{1,0:T(1,128)S(1)}, f32[1,65536]{1,0:T(1,128)S(1)}, f32[1,65536]{1,0:T(1,128)S(1)}, f32[1,65536]{1,0:T...) fusion(f32[8,65536]{1,0:T(8,128)} %all-gather.3.cloned.1.call-done), kind=kLoop, calls=%fused_computation.75 | loop fusion | bytes 4194304 | tf_op jit(solution)/shard_map/while/body/eval_jaxpr/slice | solution.py:15
  220.6 0.0 copy-start.1
  220.6 0.0 copy-start.3
  220.6 45.3 %fusion.59.clone.4 = f32[128,65536]{1,0:T(8,128)} fusion(f32[65536]{0:T(1024)S(1)} %bitcast.36, f32[128]{0:T(128)S(1)} %get-tuple-element.34, f32[65536]{0:T(1024)S(1)} %bitcast.37, f32[128]{0:T(128)S(1)} %get-tuple-element.35, f32[65536]{0:T(1024)S(1)} %bitcast.38, f32[128]{0:T(128)S(1)} %get-tuple-element.36, ...), kind=kLoop, calls=%fused_computation.1.clone.clone.clone.clone.clone.clone.clone.1 | loop fusion | flops 251658240 | bytes 35655684 | tf_op jit(solution)/shard_map/reduce_sum | solution.py:37
  265.9 114.1 %all-gather.5.cloned.1.call-done = f32[4,65536]{1,0:T(4,128)} async-done(((f32[4,128]{1,0:T(4,128)}), f32[4,65536]{1,0:T(4,128)}) %all-gather.5.cloned.1.call-update) | async-done | bytes 1048592 | tf_op jit(solution)/shard_map/all_gather | solution.py:32
  380.0 0.0 copy-done
  380.0 29.9 %multiply_reduce_fusion.1 = (f32[4]{0:T(128)S(1)}, f32[4,128]{1,0:T(4,128)S(1)}) fusion(f32[4,128]{1,0:T(4,128)S(1)} %copy-done, f32[]{:T(128)} %bitcast.34, f32[4,65536]{1,0:T(4,128)} %all-gather.5.cloned.1.call-done, f32[128,65536]{1,0:T(8,128)} %fusion.59.clone.4), kind=kOutput, calls=%fused_computation.60 | convolution fusion | flops 402655232 | bytes 34607124 | tf_op jit(solution)/shard_map/while/body/eval_jaxpr/rc,kc->kr/dot_general | solution.py:22
  409.8 102.3 %all-reduce = (f32[4]{0:T(128)S(1)}, f32[4]{0:T(128)S(1)}) all-reduce(f32[4]{0:T(128)S(1)} %multiply_reduce_fusion.2, f32[4]{0:T(128)S(1)} %get-tuple-element.43), channel_id=1, replica_groups=mesh['row'=16,'col'=32] {'row','col'}, use_global_device_ids=true, to_apply=%region_1.2 | all-reduce | flops 8 | bytes 64 | tf_op jit(solution)/shard_map/psum | solution.py:36
  512.1 0.0 copy-done.1
  512.1 0.2 multiply_reduce_fusion
  512.3 0.0 copy-start.2
  512.3 98.5 %psum.23 = f32[4]{0:T(128)S(1)} all-reduce(f32[4]{0:T(128)S(1)} %get-tuple-element.17), channel_id=1, replica_groups=mesh['row'=16,'col'=32] {'row','col'}, use_global_device_ids=true, to_apply=%region_5.6 | all-reduce | flops 4 | bytes 32 | tf_op jit(solution)/shard_map/psum | solution.py:41
  610.8 0.0 copy-done.3
  610.8 0.7 multiply_add_fusion
  611.4 0.0 copy-done.2
  (2 shorter events, 0.0 us)
Async XLA Ops:
  7.2 372.8 %copy-start = (f32[4,128]{1,0:T(4,128)S(1)}, f32[4,128]{1,0:T(4,128)}, u32[]{:S(2)}) copy-start(f32[4,128]{1,0:T(4,128)} %param.13) | copy-start | bytes 6148
  7.2 204.8 %all-gather.3.cloned.1.call-start = ((), (), s32[]{:S(2)}) async-start(), calls=%async_computation | async-start | bytes 2101248 | tf_op jit(solution)/shard_map/all_gather | solution.py:31
  8.6 371.4 %all-gather.5.cloned.1.call-start = ((), (), s32[]{:S(2)}) async-start(), calls=%async_computation.1 | async-start | bytes 1050624 | tf_op jit(solution)/shard_map/all_gather | solution.py:32
  220.6 291.5 %copy-start.1 = (f32[4,128]{1,0:T(4,128)S(1)}, f32[4,128]{1,0:T(4,128)}, u32[]{:S(2)}) copy-start(f32[4,128]{1,0:T(4,128)} %param.12) | copy-start | bytes 6148
  220.6 390.1 %copy-start.3 = (f32[4,128]{1,0:T(4,128)S(1)}, f32[4,128]{1,0:T(4,128)}, u32[]{:S(2)}) copy-start(f32[4,128]{1,0:T(4,128)} %param.11) | copy-start | bytes 6148
  512.3 99.1 %copy-start.2 = (f32[4,128]{1,0:T(4,128)}, f32[4,128]{1,0:T(4,128)S(1)}, u32[]{:S(2)}) copy-start(f32[4,128]{1,0:T(4,128)S(1)} %get-tuple-element.24) | copy-start | bytes 6148
Sparse Core Ops, SparseCore 0:
  12.6 199.3 all-gather.2
  216.6 163.3 all-gather.4
where the time goes:
time: 619 us; the launch traced here: 618 us
  waiting for transfers between devices  314 us (51%)
  blocking collectives  201 us (32%)
  other arithmetic  48.3 us (8%)
  matrix products  29.9 us (5%)
  between operations  15.4 us (2%)
  local copies, waits for them, and re-layouts  9.63 us (2%)
    all_gather x1, waiting for transfers between devices, on_device(): lax.all_gather(scaled, ('row', 'col'), axis=1, tiled=True)  200 us
    all_gather x1, waiting for transfers between devices, on_device(): lax.all_gather(direction, ('row', 'col'), axis=1, tiled=True)  114 us
    psum x1, blocking collectives, on_device(): old_rr = lax.psum(jnp.sum(residual * residual, axis=1), ('row', 'col'))  102 us
    psum x1, blocking collectives, on_device(): lax.psum(jnp.sum(new_residual * new_residual, axis=1), ('row', 'col'))  98.5 us
    reduce_sum x1, other arithmetic, on_device(): curv = lax.psum(jnp.sum(direction * image, axis=1), ('row', 'col'))  45.3 us
    dot_general x1, matrix products, one_block(): jnp.einsum('rc,kc->kr', values, col_dir, precision=lax.Precision.HIGHEST)  29.9 us
  transfers between devices with their start and end apart: 2, of which 2 were waited for; matrix products, arithmetic and copies ran while one was open for 9% of the time, Pallas kernels for 0%

commit v1 on v0

v1 whole, which is shorter than its diff:
```python
import functools
import math

import jax
import jax.numpy as jnp
from jax import lax
from jax.experimental import pallas as pl
from jax.experimental.pallas import tpu as pltpu
from jax.sharding import Mesh, PartitionSpec as P

BLK = 128
LN2 = math.log(2.0)
UNIT = math.sqrt(5.0) / LN2
HALF = 1.5 / LN2
REST = 3.0 / LN2**2 - HALF**2
FRONT = LN2**2 / 3.0
TINY = 1e-12
FEAT = 64


def round16(x):
    return x.astype(jnp.bfloat16).astype(jnp.float32)


def split3(x):
    first = round16(x)
    rest = x - first
    second = round16(rest)
    return first, second, round16(rest - second)


def norm_rows(pts, flip):
    parts = split3(jnp.sum(pts * pts, axis=0, keepdims=True))
    row = lax.broadcasted_iota(jnp.int32, pts.shape, 0)
    at = 3 if flip else 0
    out = jnp.where((row >= 3 - at) & (row < 6 - at), 1.0, 0.0)
    for k in range(3):
        out = jnp.where(row == at + k, parts[k], out)
    return out


def out_features(pts):
    a, b, c = split3(pts)
    return jnp.concatenate([a, b, c, a, b, a, norm_rows(pts, False), jnp.zeros_like(pts)], 0)


def in_features(pts):
    a, b, c = split3(-2.0 * pts)
    return jnp.concatenate([a, a, a, b, b, c, norm_rows(pts, True), jnp.zeros_like(pts)], 0)


def product_kernel(tb, sb, s_ref, t_ref, out_ref, g_ref, f_ref, d_ref, acc_ref):
    n_s, n_t = s_ref.shape[0], t_ref.shape[0]
    for k in range(n_s):
        g_ref[:, k * BLK : (k + 1) * BLK] = out_features(s_ref[k, :8, :]).astype(jnp.bfloat16)
    for k in range(n_t):
        at = slice(k * BLK, (k + 1) * BLK)
        rows = in_features(t_ref[k, :8, :])
        f_ref[at, :] = jnp.transpose(rows).astype(jnp.bfloat16)
        a, b, c = split3(t_ref[k, 8:12, :])
        d_ref[:, at] = jnp.concatenate([a, b, c, jnp.zeros_like(a)], 0).astype(jnp.bfloat16)
    acc_ref[...] = jnp.zeros_like(acc_ref)

    def step(i, carry):
        t_at = pl.ds(pl.multiple_of(i * tb, tb), tb)
        left = f_ref[t_at, :]
        weights = d_ref[:, t_at]
        for j in range(n_s * BLK // sb):
            s_at = slice(j * sb, (j + 1) * sb)
            d2 = jnp.dot(left, g_ref[:, s_at], preferred_element_type=jnp.float32)
            d2 = jnp.maximum(d2, TINY)
            neg = -(d2 * lax.rsqrt(d2))
            shifted = neg - HALF
            value = (shifted * shifted + REST) * jnp.exp2(neg)
            high = value.astype(jnp.bfloat16)
            low = (value - high.astype(jnp.float32)).astype(jnp.bfloat16)
            acc_ref[:, s_at] += jnp.dot(
                weights, high, preferred_element_type=jnp.float32
            ) + jnp.dot(weights, low, preferred_element_type=jnp.float32)
        return carry

    lax.fori_loop(0, n_t * BLK // tb, step, 0)
    total = acc_ref[0:4, :] + acc_ref[4:8, :] + acc_ref[8:12, :]
    for k in range(n_s):
        out_ref[k, :, :] = total[:, k * BLK : (k + 1) * BLK]


def kernel_product(s_blocks, t_blocks, tb=256, sb=512):
    n_s, n_t = s_blocks.shape[0], t_blocks.shape[0]
    return pl.pallas_call(
        functools.partial(product_kernel, tb, sb),
        out_shape=jax.ShapeDtypeStruct((n_s, 4, BLK), jnp.float32),
        in_specs=[pl.BlockSpec(memory_space=pltpu.VMEM)] * 2,
        out_specs=pl.BlockSpec(memory_space=pltpu.VMEM),
        scratch_shapes=[
            pltpu.VMEM((FEAT, n_s * BLK), jnp.bfloat16),
            pltpu.VMEM((n_t * BLK, FEAT), jnp.bfloat16),
            pltpu.VMEM((16, n_t * BLK), jnp.bfloat16),
            pltpu.VMEM((16, n_s * BLK), jnp.float32),
        ],
        compiler_params=pltpu.CompilerParams(vmem_limit_bytes=32 * 1024 * 1024),
    )(s_blocks, t_blocks)


def tiled(x, n):
    return jnp.broadcast_to(x[None], (n,) + x.shape)


def on_device(points, lengthscale, signal_var, noise_var, solution, residual, direction):
    scaled = points / lengthscale[:, None] * UNIT
    mine = jnp.concatenate([scaled, direction, residual], 0)
    with jax.named_scope("gather_out_points"):
        s_blocks = lax.all_to_all(tiled(mine, 16), "row", 0, 0)
    with jax.named_scope("gather_in_points"):
        t_half = lax.all_to_all(tiled(mine[:12], 16), "z", 0, 0)
        t_other = lax.ppermute(t_half, "core", [(0, 1), (1, 0)])
    part = kernel_product(s_blocks, jnp.concatenate([t_half, t_other], 0))
    with jax.named_scope("sum_partial_images"):
        applied = jnp.sum(lax.all_to_all(tiled(part, 16), "row", 0, 0), 0)
    s_dir, s_res = s_blocks[:, 8:12], s_blocks[:, 12:16]
    image = (signal_var[0] * FRONT) * applied + noise_var[0] * s_dir
    sums = jnp.concatenate(
        [
            jnp.sum(u * v, (0, 2))
            for u, v in ((s_res, s_res), (s_dir, image), (s_res, image), (image, image))
        ]
    )
    with jax.named_scope("sum_scalars"):
        sums = lax.all_to_all(tiled(jnp.pad(sums, (0, 112))[None], 32), ("z", "core"), 0, 0)
    sums = jnp.sum(sums, (0, 1))
    old_rr, curv, res_image, image_sq = (sums[4 * k : 4 * k + 4, None] for k in range(4))
    own = lax.dynamic_index_in_dim(image, lax.axis_index("row"), 0, False)
    alpha = old_rr / curv
    new_rr = old_rr - 2.0 * alpha * res_image + alpha * alpha * image_sq
    new_solution = solution + alpha * direction
    new_residual = residual - alpha * own
    new_direction = new_residual + (new_rr / old_rr) * direction
    return new_solution, new_residual, new_direction


def solution(mesh):
    fine = Mesh(mesh.devices.reshape(16, 16, 2), ("row", "z", "core"))
    cut = P(None, ("row", "z", "core"))
    return jax.shard_map(
        on_device,
        mesh=fine,
        in_specs=(cut, P(), P(), P(), cut, cut, cut),
        out_specs=(cut, cut, cut),
        check_vma=False,
    )
```

time: 619 us -> 112 us (0.18)
  waiting for transfers between devices: 314 us -> 27.8 us
  blocking collectives: 201 us -> 27.5 us
  other arithmetic: 48.3 us -> 1.85 us
  matrix products: 29.9 us -> 0 us
  Pallas kernels: 0 us -> 27.6 us
  starting transfers between devices: 0.08 us -> 22 us
  between operations: 15.4 us -> 2.04 us
  local copies, waits for them, and re-layouts: 9.63 us -> 2.81 us
    all_gather x2 -> x0, waiting for transfers between devices: 314 us -> none  [the longest x1 200 us: on_device(): lax.all_gather(scaled, ('row', 'col'), axis=1, tiled=True)]
    psum x2 -> x0, blocking collectives: 201 us -> none  [the longest x1 102 us: on_device(): old_rr = lax.psum(jnp.sum(residual * residual, axis=1), ('row', 'col'))]
    reduce_sum x3, other arithmetic: 46.3 us -> 0.24 us  [the longest x1 0.18 us: on_device(): jnp.sum(u * v, (0, 2))]
    dot_general x1 -> x0, matrix products: 29.9 us -> none  [one_block(): jnp.einsum('rc,kc->kr', values, col_dir, precision=lax.Precision.HIGHEST)]
    all_to_all x0 -> x3, waiting for transfers between devices: none -> 27.8 us  [the longest x1 11.7 us: on_device(): lax.all_to_all(tiled(jnp.pad(sums, (0, 112))[None], 32), ('z', 'core'), 0...]
    pallas_call x0 -> x1, Pallas kernels: none -> 27.6 us  [kernel_product(): pl.pallas_call(functools.partial(product_kernel, tb, sb), out_shape=jax.S...]
    all_to_all x0 -> x1, blocking collectives: none -> 27.5 us  [on_device(): t_half = lax.all_to_all(tiled(mine[:12], 16), 'z', 0, 0)]
    all_to_all x0 -> x3, starting transfers between devices: none -> 16.5 us  [the longest x1 6.75 us: on_device(): s_blocks = lax.all_to_all(tiled(mine, 16), 'row', 0, 0)]
  transfers between devices with their start and end apart: 2 -> 4, of which waited for: 2 -> 3; matrix products, arithmetic and copies ran while one was open for 9% -> 1% of each run, Pallas kernels for 0% -> 0%
where the time goes in v1:
time: 112 us
  waiting for transfers between devices  27.8 us (25%)
  Pallas kernels  27.6 us (25%)
  blocking collectives  27.5 us (25%)
  starting transfers between devices  22 us (20%)
  local copies, waits for them, and re-layouts  2.81 us (3%)
  between operations  2.04 us (2%)
  other arithmetic  1.85 us (2%)
    pallas_call x1, Pallas kernels, kernel_product(): pl.pallas_call(functools.partial(product_kernel, tb, sb), out_shape=jax.S...  27.6 us
    all_to_all x1, blocking collectives, on_device(): t_half = lax.all_to_all(tiled(mine[:12], 16), 'z', 0, 0)  27.5 us
    all_to_all x1, waiting for transfers between devices, on_device(): lax.all_to_all(tiled(jnp.pad(sums, (0, 112))[None], 32), ('z', 'core'), 0...  11.7 us
    all_to_all x1, waiting for transfers between devices, on_device(): applied = jnp.sum(lax.all_to_all(tiled(part, 16), 'row', 0, 0), 0)  9 us
    all_to_all x1, waiting for transfers between devices, on_device(): s_blocks = lax.all_to_all(tiled(mine, 16), 'row', 0, 0)  7.1 us
    all_to_all x1, starting transfers between devices, on_device(): s_blocks = lax.all_to_all(tiled(mine, 16), 'row', 0, 0)  6.75 us
    all_to_all x1, starting transfers between devices, on_device(): lax.all_to_all(tiled(jnp.pad(sums, (0, 112))[None], 32), ('z', 'core'), 0...  6.17 us
    ppermute x1, starting transfers between devices, on_device(): t_other = lax.ppermute(t_half, 'core', [(0, 1), (1, 0)])  5.55 us
  transfers between devices with their start and end apart: 4, of which 3 were waited for; matrix products, arithmetic and copies ran while one was open for 1% of the time, Pallas kernels for 0%

profile of v1, /device:TPU:1, one launch (start us, length us, event | category | flops | bytes accessed | tf_op | source)
XLA Modules:
  0.0 111.8 jit_solution(9339307887997378423)
XLA Ops:
  0.6 0.0 copy-start
  0.6 0.8 divide_multiply_fusion
  1.4 0.0 copy-done
  1.4 0.0 copy-start.1
  1.5 27.5 %all_to_all.20 = f32[16,12,128]{2,1,0:T(8,128)S(1)} all-to-all(f32[16,12,128]{2,1,0:T(8,128)S(1)} %broadcast_in_dim.9), channel_id=1, replica_groups=mesh['row'=16,'z'=16,'core'=2] {'z'}, dimensions={0} | all-to-all | bytes 196608 | tf_op jit(solution)/shard_map/gather_in_points/all_to_all | solution.py:115
  29.0 5.6 %collective-permute-start = (f32[16,12,128]{2,1,0:T(8,128)S(1)}, f32[16,12,128]{2,1,0:T(8,128)S(1)}, u32[]{:S(2)}, u32[]{:S(2)}) collective-permute-start(f32[16,12,128]{2,1,0:T(8,128)S(1)} %all_to_all.20), channel_id=1, source_target_pairs={{0,1},{1,0},{2,3},{3,2},{4,5},{5,4},{6,7},{7,6},{8,9},{9,8},{10,11... | collective-permute-start | bytes 294920 | tf_op jit(solution)/shard_map/gather_in_points/ppermute | solution.py:116
  34.6 0.0 copy-done.1
  34.6 0.6 broadcast_in_dim.8
  35.2 6.8 %all-to-all-start = ((f32[16,16,128]{2,1,0:T(8,128)}), f32[16,16,128]{2,1,0:T(8,128)S(1)}, u32[]{:S(2)}, u32[]{:S(2)}) async-start(f32[16,16,128]{2,1,0:T(8,128)} %broadcast_in_dim.8), calls=%async_computation | async-start | bytes 262144 | tf_op jit(solution)/shard_map/gather_out_points/all_to_all | solution.py:113
  42.0 0.0 collective-permute-done
  42.0 7.1 %all-to-all-done.s_ref = f32[16,16,128]{2,1,0:T(8,128)S(1)} async-done(((f32[16,16,128]{2,1,0:T(8,128)}), f32[16,16,128]{2,1,0:T(8,128)S(1)}, u32[]{:S(2)}, u32[]{:S(2)}) %all-to-all-start) | async-done | bytes 131104 | tf_op jit(solution)/shard_map/gather_out_points/all_to_all | solution.py:113
  49.1 27.6 %shard_map.94 = f32[16,4,128]{2,1,0:T(4,128)S(1)} custom-call(f32[16,16,128]{2,1,0:T(8,128)S(1)} %all-to-all-done.s_ref, f32[32,12,128]{2,1,0:T(8,128)S(1)} %pad_maximum_fusion.t_ref), custom_call_target="tpu_custom_call" | custom-call | tf_op jit(solution)/shard_map/pallas_call | solution.py:90
  76.8 0.8 broadcast_in_dim.10
  77.6 3.6 %all-to-all-start.2 = ((f32[16,16,4,128]{3,1,2,0:T(8,128)}), f32[16,16,4,128]{3,1,2,0:T(8,128)S(1)}, u32[]{:S(2)}, u32[]{:S(2)}) async-start(f32[16,16,4,128]{3,1,2,0:T(8,128)} %broadcast_in_dim.10), calls=%async_computation.2 | async-start | bytes 1048576 | tf_op jit(solution)/shard_map/sum_partial_images/all_to_all | solution.py:119
  82.5 9.0 %all-to-all-done.2 = f32[16,16,4,128]{3,1,2,0:T(8,128)S(1)} async-done(((f32[16,16,4,128]{3,1,2,0:T(8,128)}), f32[16,16,4,128]{3,1,2,0:T(8,128)S(1)}, u32[]{:S(2)}, u32[]{:S(2)}) %all-to-all-start.2) | async-done | bytes 524320 | tf_op jit(solution)/shard_map/sum_partial_images/all_to_all | solution.py:119
  91.5 0.2 multiply_reduce_fusion.2
  91.7 0.1 select_maximum_fusion
  91.8 0.6 broadcast_in_dim.11
  92.4 6.2 %all-to-all-start.3 = ((f32[32,1,128]{2,1,0:T(1,128)}), f32[32,1,128]{2,1,0:T(1,128)S(1)}, u32[]{:S(2)}, u32[]{:S(2)}) async-start(f32[32,1,128]{2,1,0:T(1,128)} %broadcast_in_dim.11), calls=%async_computation.3 | async-start | bytes 32768 | tf_op jit(solution)/shard_map/sum_scalars/all_to_all | solution.py:129
  98.6 11.7 %all-to-all-done.3 = f32[32,1,128]{2,1,0:T(1,128)S(1)} async-done(((f32[32,1,128]{2,1,0:T(1,128)}), f32[32,1,128]{2,1,0:T(1,128)S(1)}, u32[]{:S(2)}, u32[]{:S(2)}) %all-to-all-start.3) | async-done | bytes 16416 | tf_op jit(solution)/shard_map/sum_scalars/all_to_all | solution.py:129
  110.4 0.1 add_divide_fusion
  110.4 0.0 copy-start.2
  110.4 0.7 copy-done.2
  111.1 0.7 multiply_add_fusion
  (7 shorter events, 0.1 us)
Async XLA Ops:
  0.6 0.8 copy-start
  1.4 33.1 %copy-start.1 = (f32[4,128]{1,0:T(4,128)S(1)}, f32[4,128]{1,0:T(4,128)}, u32[]{:S(2)}) copy-start(f32[4,128]{1,0:T(4,128)} %param.12) | copy-start | bytes 6148
  29.0 13.0 %collective-permute-start = (f32[16,12,128]{2,1,0:T(8,128)S(1)}, f32[16,12,128]{2,1,0:T(8,128)S(1)}, u32[]{:S(2)}, u32[]{:S(2)}) collective-permute-start(f32[16,12,128]{2,1,0:T(8,128)S(1)} %all_to_all.20), channel_id=1, source_target_pairs={{0,1},{1,0},{2,3},{3,2},{4,5},{5,4},{6,7},{7,6},{8,9},{9,8},{10,11... | collective-permute-start | bytes 294920 | tf_op jit(solution)/shard_map/gather_in_points/ppermute | solution.py:116
  35.2 13.9 %all-to-all-start = ((f32[16,16,128]{2,1,0:T(8,128)}), f32[16,16,128]{2,1,0:T(8,128)S(1)}, u32[]{:S(2)}, u32[]{:S(2)}) async-start(f32[16,16,128]{2,1,0:T(8,128)} %broadcast_in_dim.8), calls=%async_computation | async-start | bytes 262144 | tf_op jit(solution)/shard_map/gather_out_points/all_to_all | solution.py:113
  77.6 13.9 %all-to-all-start.2 = ((f32[16,16,4,128]{3,1,2,0:T(8,128)}), f32[16,16,4,128]{3,1,2,0:T(8,128)S(1)}, u32[]{:S(2)}, u32[]{:S(2)}) async-start(f32[16,16,4,128]{3,1,2,0:T(8,128)} %broadcast_in_dim.10), calls=%async_computation.2 | async-start | bytes 1048576 | tf_op jit(solution)/shard_map/sum_partial_images/all_to_all | solution.py:119
  92.4 17.9 %all-to-all-start.3 = ((f32[32,1,128]{2,1,0:T(1,128)}), f32[32,1,128]{2,1,0:T(1,128)S(1)}, u32[]{:S(2)}, u32[]{:S(2)}) async-start(f32[32,1,128]{2,1,0:T(1,128)} %broadcast_in_dim.11), calls=%async_computation.3 | async-start | bytes 32768 | tf_op jit(solution)/shard_map/sum_scalars/all_to_all | solution.py:129
  110.4 0.7 copy-start.2

commit v2 on v1

v2 whole, which is shorter than its diff:
```python
import functools
import math

import jax
import jax.numpy as jnp
from jax import lax
from jax.experimental import pallas as pl
from jax.experimental.pallas import tpu as pltpu
from jax.sharding import Mesh, PartitionSpec as P

BLK = 128
LN2 = math.log(2.0)
UNIT = math.sqrt(5.0) / LN2
HALF = 1.5 / LN2
REST = 3.0 / LN2**2 - HALF**2
FRONT = LN2**2 / 3.0
TINY = 1e-12
FEAT = 64
QUARTER = 16
S_TILE = 256


def round16(x):
    return x.astype(jnp.bfloat16).astype(jnp.float32)


def split3(x):
    first = round16(x)
    rest = x - first
    second = round16(rest)
    return first, second, round16(rest - second)


def norm_rows(pts, flip):
    parts = split3(jnp.sum(pts * pts, axis=0, keepdims=True))
    row = lax.broadcasted_iota(jnp.int32, pts.shape, 0)
    at = 3 if flip else 0
    out = jnp.where((row >= 3 - at) & (row < 6 - at), 1.0, 0.0)
    for k in range(3):
        out = jnp.where(row == at + k, parts[k], out)
    return out


def out_features(pts):
    a, b, c = split3(pts)
    return jnp.concatenate([a, b, c, a, b, a, norm_rows(pts, False), jnp.zeros_like(pts)], 0)


def in_features(pts):
    a, b, c = split3(-2.0 * pts)
    return jnp.concatenate([a, a, a, b, b, c, norm_rows(pts, True), jnp.zeros_like(pts)], 0)


def product_kernel(first, last, y_ref, s_ref, t_ref, prior_ref, out_ref, g_ref, f_ref, d_ref, acc_ref):
    n_s = s_ref.shape[0]
    for k in range(n_s):
        g_ref[:, k * BLK : (k + 1) * BLK] = out_features(s_ref[k, :8, :]).astype(jnp.bfloat16)
    acc_ref[...] = jnp.zeros_like(acc_ref)
    me = y_ref[0]

    def step(i, carry):
        quarter = lax.rem(me + i, t_ref.shape[0])
        for k in range(QUARTER):
            at = slice(k * BLK, (k + 1) * BLK)
            rows = in_features(t_ref[quarter, k, :8, :])
            f_ref[at, :] = jnp.transpose(rows).astype(jnp.bfloat16)
            a, b, c = split3(t_ref[quarter, k, 8:12, :])
            d_ref[:, at] = jnp.concatenate([a, b, c, jnp.zeros_like(a)], 0).astype(jnp.bfloat16)
        left = f_ref[...]
        weights = d_ref[...]
        for j in range(n_s * BLK // S_TILE):
            at = slice(j * S_TILE, (j + 1) * S_TILE)
            d2 = jnp.dot(left, g_ref[:, at], preferred_element_type=jnp.float32)
            d2 = jnp.maximum(d2, TINY)
            neg = -(d2 * lax.rsqrt(d2))
            shifted = neg - HALF
            value = (shifted * shifted + REST) * jnp.exp2(neg)
            high = value.astype(jnp.bfloat16)
            low = (value - high.astype(jnp.float32)).astype(jnp.bfloat16)
            acc_ref[:, at] += jnp.dot(
                weights, high, preferred_element_type=jnp.float32
            ) + jnp.dot(weights, low, preferred_element_type=jnp.float32)
        return carry

    lax.fori_loop(first, last, step, 0)
    total = acc_ref[0:4, :] + acc_ref[4:8, :] + acc_ref[8:12, :]
    for k in range(n_s):
        out_ref[k, :, :] = prior_ref[k, :, :] + total[:, k * BLK : (k + 1) * BLK]


def kernel_product(me, s_blocks, t_blocks, prior, first, last):
    n_s = s_blocks.shape[0]
    entries = (last - first) * QUARTER * BLK * n_s * BLK
    return pl.pallas_call(
        functools.partial(product_kernel, first, last),
        out_shape=jax.ShapeDtypeStruct((n_s, 4, BLK), jnp.float32),
        in_specs=[pl.BlockSpec(memory_space=pltpu.SMEM)]
        + [pl.BlockSpec(memory_space=pltpu.VMEM)] * 3,
        out_specs=pl.BlockSpec(memory_space=pltpu.VMEM),
        scratch_shapes=[
            pltpu.VMEM((FEAT, n_s * BLK), jnp.bfloat16),
            pltpu.VMEM((QUARTER * BLK, FEAT), jnp.bfloat16),
            pltpu.VMEM((16, QUARTER * BLK), jnp.bfloat16),
            pltpu.VMEM((16, n_s * BLK), jnp.float32),
        ],
        compiler_params=pltpu.CompilerParams(vmem_limit_bytes=40 * 1024 * 1024),
        cost_estimate=pl.CostEstimate(
            flops=entries * 192, bytes_accessed=0, transcendentals=entries * 2
        ),
    )(me, s_blocks, t_blocks, prior)


def tiled(x, n):
    return jnp.broadcast_to(x[None], (n,) + x.shape)


AXIS = "d"
YS, XS, ZS, CS = (2, 3, 0, 1), (2, 3, 0, 1), tuple((8 + k) % 16 for k in range(16)), (0, 1)


def flat(y, x, z, c):
    return ((y * 4 + x) * 16 + z) * 2 + c


ALONG_Z = [[flat(y, x, z, c) for z in ZS] for y in YS for x in XS for c in CS]
ALONG_Y = [[flat(y, x, z, c) for y in YS] for x in XS for z in ZS for c in CS]
ALONG_XC = [[flat(y, x, z, c) for x in XS for c in CS] for y in YS for z in ZS]
ALONG_YZ = [[flat(y, x, z, c) for y in YS for z in ZS] for x in XS for c in CS]
EVERY = [(y, x, z, c) for y in range(4) for x in range(4) for z in range(16) for c in range(2)]


def share(x, groups):
    return lax.all_to_all(x, AXIS, 0, 0, axis_index_groups=groups)


def shift_x(v, by):
    return lax.ppermute(
        v, AXIS, [(flat(y, x, z, c), flat(y, (x - by) % 4, z, c)) for y, x, z, c in EVERY]
    )


def swap_core(v):
    return lax.ppermute(v, AXIS, [(i, i ^ 1) for i in range(512)])


def on_device(points, lengthscale, signal_var, noise_var, solution, residual, direction):
    here = lax.axis_index(AXIS)
    at_y, at_x, core = here // 128, here // 32 % 4, here % 2
    scaled = points / lengthscale[:, None] * UNIT
    mine = jnp.concatenate([scaled, direction, residual], 0)
    with jax.named_scope("gather_in_points_z"):
        t_quarter = share(tiled(mine[:12], 16), ALONG_Z)
    with jax.named_scope("gather_out_points"):
        row = jnp.stack([mine] + [shift_x(mine, k) for k in (1, 2, 3)])
        row = jnp.roll(row, at_x, 0)
        swapped = swap_core(row)
        s_blocks = jnp.concatenate(
            [jnp.where(core == 0, row, swapped), jnp.where(core == 0, swapped, row)], 0
        )
    with jax.named_scope("gather_in_points_y"):
        t_all = share(tiled(t_quarter, 4), ALONG_Y)
    me = (at_y + 2)[None] % 4
    part = kernel_product(
        jnp.zeros_like(me), s_blocks, t_quarter[None], jnp.zeros((8, 4, BLK), jnp.float32), 0, 1
    )
    part = kernel_product(me, s_blocks, t_all, part, 1, 4)
    with jax.named_scope("sum_partial_images"):
        applied = jnp.sum(share(tiled(part, 8), ALONG_XC), 0)
    s_dir, s_res = s_blocks[:, 8:12], s_blocks[:, 12:16]
    image = (signal_var[0] * FRONT) * applied + noise_var[0] * s_dir
    sums = jnp.concatenate(
        [
            jnp.sum(u * v, (0, 2))
            for u, v in ((s_res, s_res), (s_dir, image), (s_res, image), (image, image))
        ]
    )
    with jax.named_scope("sum_scalars"):
        sums = share(tiled(jnp.pad(sums, (0, 112))[None], 64), ALONG_YZ)
    sums = jnp.sum(sums, (0, 1))
    old_rr, curv, res_image, image_sq = (sums[4 * k : 4 * k + 4, None] for k in range(4))
    own = lax.dynamic_index_in_dim(image, core * 4 + at_x, 0, False)
    alpha = old_rr / curv
    new_rr = old_rr - 2.0 * alpha * res_image + alpha * alpha * image_sq
    new_solution = solution + alpha * direction
    new_residual = residual - alpha * own
    new_direction = new_residual + (new_rr / old_rr) * direction
    return new_solution, new_residual, new_direction


def solution(mesh):
    line = Mesh(mesh.devices.reshape(-1), (AXIS,))
    cut = P(None, AXIS)
    return jax.shard_map(
        on_device,
        mesh=line,
        in_specs=(cut, P(), P(), P(), cut, cut, cut),
        out_specs=(cut, cut, cut),
        check_vma=False,
    )
```

time: 112 us -> 92.7 us (0.83); the launches traced: 112 us -> 91.3 us
  starting transfers between devices: 22 us -> 61.2 us
  blocking collectives: 27.5 us -> 0 us
  waiting for transfers between devices: 27.8 us -> 4.31 us
  Pallas kernels: 27.6 us -> 18.1 us
    all_to_all x3 -> x4, starting transfers between devices: 16.5 us -> 47.1 us  [share(): return lax.all_to_all(x, AXIS, 0, 0, axis_index_groups=groups)]
    all_to_all x1 -> x0, blocking collectives: 27.5 us -> none  [on_device(): t_half = lax.all_to_all(tiled(mine[:12], 16), 'z', 0, 0)]
    all_to_all x3 -> x4, waiting for transfers between devices: 27.8 us -> 4.3 us  [share(): return lax.all_to_all(x, AXIS, 0, 0, axis_index_groups=groups)]
    pallas_call x1 -> x2, Pallas kernels: 27.6 us -> 18.1 us  [kernel_product(): pl.pallas_call(functools.partial(product_kernel, first, last), out_shape=...]
    ppermute x1 -> x4, starting transfers between devices: 5.55 us -> 14.1 us  [the longest x3 10.2 us: shift_x(): lax.ppermute(v, AXIS, [(flat(y, x, z, c), flat(y, (x - by) % 4, z, c)) fo...]
  transfers between devices with their start and end apart: 4 -> 8, of which waited for: 3 -> 3; matrix products, arithmetic and copies ran while one was open for 1% -> 2% of each run, Pallas kernels for 0% -> 5%
where the time goes in v2:
time: 92.7 us; the launch traced here: 91.3 us
  starting transfers between devices  61.2 us (66%)
  Pallas kernels  18.1 us (20%)
  waiting for transfers between devices  4.31 us (5%)
  local copies, waits for them, and re-layouts  3.6 us (4%)
  between operations  2.25 us (2%)
  other arithmetic  1.84 us (2%)
    all_to_all x4, starting transfers between devices, share(): return lax.all_to_all(x, AXIS, 0, 0, axis_index_groups=groups)  47.1 us
    pallas_call x2, Pallas kernels, kernel_product(): pl.pallas_call(functools.partial(product_kernel, first, last), out_shape=...  18.1 us
    ppermute x3, starting transfers between devices, shift_x(): lax.ppermute(v, AXIS, [(flat(y, x, z, c), flat(y, (x - by) % 4, z, c)) fo...  10.2 us
    all_to_all x4, waiting for transfers between devices, share(): return lax.all_to_all(x, AXIS, 0, 0, axis_index_groups=groups)  4.3 us
    ppermute x1, starting transfers between devices, swap_core(): return lax.ppermute(v, AXIS, [(i, i ^ 1) for i in range(512)])  3.98 us
    broadcast_in_dim x4, local copies, waits for them, and re-layouts, tiled(): return jnp.broadcast_to(x[None], (n,) + x.shape)  2.7 us
  transfers between devices with their start and end apart: 8, of which 3 were waited for; matrix products, arithmetic and copies ran while one was open for 2% of the time, Pallas kernels for 5%

profile of v2, /device:TPU:1, one launch (start us, length us, event | category | flops | bytes accessed | tf_op | source)
XLA Modules:
  0.0 91.3 jit_solution(2930619829983613024)
XLA Ops:
  0.6 0.0 copy-start.1
  0.6 0.0 copy-start
  0.7 0.8 divide_multiply_fusion
  1.4 0.0 copy-done.1
  1.4 0.0 copy-done
  1.4 5.2 %collective-permute-start = (f32[16,128]{1,0:T(8,128)S(1)}, f32[16,128]{1,0:T(8,128)S(1)}, u32[]{:S(2)}, u32[]{:S(2)}) collective-permute-start(f32[16,128]{1,0:T(8,128)S(1)} %pad_maximum_fusion.1), channel_id=1, source_target_pairs={{0,96},{1,97},{2,98},{3,99},{4,100},{5,101},{6,102},{7,103},{8,104... | collective-permute-start | bytes 24584 | tf_op jit(solution)/shard_map/gather_out_points/ppermute | solution.py:137
  6.7 2.4 %collective-permute-start.1 = (f32[16,128]{1,0:T(8,128)S(1)}, f32[16,128]{1,0:T(8,128)S(1)}, u32[]{:S(2)}, u32[]{:S(2)}) collective-permute-start(f32[16,128]{1,0:T(8,128)S(1)} %pad_maximum_fusion.1), channel_id=1, source_target_pairs={{0,64},{1,65},{2,66},{3,67},{4,68},{5,69},{6,70},{7,71},{8,72},{9,... | collective-permute-start | bytes 24584 | tf_op jit(solution)/shard_map/gather_out_points/ppermute | solution.py:137
  9.1 2.5 %collective-permute-start.2 = (f32[16,128]{1,0:T(8,128)S(1)}, f32[16,128]{1,0:T(8,128)S(1)}, u32[]{:S(2)}, u32[]{:S(2)}) collective-permute-start(f32[16,128]{1,0:T(8,128)S(1)} %pad_maximum_fusion.1), channel_id=1, source_target_pairs={{0,32},{1,33},{2,34},{3,35},{4,36},{5,37},{6,38},{7,39},{8,40},{9,... | collective-permute-start | bytes 24584 | tf_op jit(solution)/shard_map/gather_out_points/ppermute | solution.py:137
  11.6 0.6 broadcast_in_dim.15
  12.3 18.3 %all-to-all-start = ((f32[16,12,128]{2,1,0:T(8,128)}), f32[16,12,128]{2,1,0:T(8,128)S(1)}, u32[]{:S(2)}, u32[]{:S(2)}) async-start(f32[16,12,128]{2,1,0:T(8,128)} %broadcast_in_dim.15), calls=%async_computation | async-start | bytes 262144 | tf_op jit(solution)/shard_map/gather_in_points_z/all_to_all | solution.py:133
  30.6 0.0 collective-permute-done
  30.7 0.0 collective-permute-done.1
  30.7 0.0 collective-permute-done.2
  30.8 4.0 %collective-permute-start.3 = (f32[4,16,128]{2,1,0:T(8,128)S(1)}, f32[4,16,128]{2,1,0:T(8,128)S(1)}, u32[]{:S(2)}, u32[]{:S(2)}) collective-permute-start(f32[4,16,128]{2,1,0:T(8,128)S(1)} %constant_dynamic-slice_fusion), channel_id=1, source_target_pairs={{0,1},{1,0},{2,3},{3,2},{4,5},{5,4},{6,7},{7,6},{8,9},{9,8},{10,11... | collective-permute-start | bytes 98312 | tf_op jit(solution)/shard_map/gather_out_points/ppermute | solution.py:143
  34.8 1.4 %all-to-all-done = f32[16,12,128]{2,1,0:T(8,128)S(1)} async-done(((f32[16,12,128]{2,1,0:T(8,128)}), f32[16,12,128]{2,1,0:T(8,128)S(1)}, u32[]{:S(2)}, u32[]{:S(2)}) %all-to-all-start) | async-done | bytes 98336 | tf_op jit(solution)/shard_map/gather_in_points_z/all_to_all | solution.py:133
  36.3 0.8 broadcast_in_dim.16
  37.1 6.3 %all-to-all-start.1 = ((f32[4,16,12,128]{3,1,2,0:T(8,128)}), f32[4,16,12,128]{3,1,2,0:T(8,128)S(1)}, u32[]{:S(2)}, u32[]{:S(2)}) async-start(f32[4,16,12,128]{3,1,2,0:T(8,128)} %broadcast_in_dim.16), calls=%async_computation.1 | async-start | bytes 786432 | tf_op jit(solution)/shard_map/gather_in_points_y/all_to_all | solution.py:133
  43.4 0.0 collective-permute-done.3
  43.4 4.5 %shard_map.94.prior_ref = f32[8,4,128]{2,1,0:T(4,128)S(1)} custom-call(s32[1]{0:T(128)} %constant.96.clone.1.y_ref, f32[8,16,128]{2,1,0:T(8,128)S(1)} %pad_maximum_fusion.s_ref, f32[1,16,12,128]{3,2,1,0:T(8,128)S(1)} %bitcast.23, f32[8,4,128]{2,1,0:T(4,128)S(1)} %broadcast_in_dim.18.prior_ref), custom_call_target="tpu_custom_call" | custom-call | flops 402653184 | tf_op jit(solution)/shard_map/pallas_call | solution.py:94
  48.0 0.0 all-to-all-done.1
  48.0 0.1 copy.17.t_ref
  48.1 13.6 %shard_map.95 = f32[8,4,128]{2,1,0:T(4,128)S(1)} custom-call(s32[1]{0:T(128)S(6)} %select_n.61.y_ref, f32[8,16,128]{2,1,0:T(8,128)S(1)} %pad_maximum_fusion.s_ref, f32[4,16,12,128]{3,2,1,0:T(8,128)S(1)} %copy.17.t_ref, f32[8,4,128]{2,1,0:T(4,128)S(1)} %shard_map.94.prior_ref), custom_call_target="tpu_custom_call" | custom-call | flops 1207959552 | tf_op jit(solution)/shard_map/pallas_call | solution.py:94
  61.7 0.6 broadcast_in_dim.19
  62.4 7.4 %all-to-all-start.2 = ((f32[8,8,4,128]{3,1,2,0:T(8,128)}), f32[8,8,4,128]{3,1,2,0:T(8,128)S(1)}, u32[]{:S(2)}, u32[]{:S(2)}) async-start(f32[8,8,4,128]{3,1,2,0:T(8,128)} %broadcast_in_dim.19), calls=%async_computation.2 | async-start | bytes 262144 | tf_op jit(solution)/shard_map/sum_partial_images/all_to_all | solution.py:133
  71.1 1.2 %all-to-all-done.2 = f32[8,8,4,128]{3,1,2,0:T(8,128)S(1)} async-done(((f32[8,8,4,128]{3,1,2,0:T(8,128)}), f32[8,8,4,128]{3,1,2,0:T(8,128)S(1)}, u32[]{:S(2)}, u32[]{:S(2)}) %all-to-all-start.2) | async-done | bytes 131104 | tf_op jit(solution)/shard_map/sum_partial_images/all_to_all | solution.py:133
  72.4 0.2 multiply_reduce_fusion.2
  72.5 0.1 select_maximum_fusion
  72.6 0.6 broadcast_in_dim.20
  73.2 15.0 %all-to-all-start.3 = ((f32[64,1,128]{2,1,0:T(1,128)}), f32[64,1,128]{2,1,0:T(1,128)S(1)}, u32[]{:S(2)}, u32[]{:S(2)}) async-start(f32[64,1,128]{2,1,0:T(1,128)} %broadcast_in_dim.20), calls=%async_computation.3 | async-start | bytes 65536 | tf_op jit(solution)/shard_map/sum_scalars/all_to_all | solution.py:133
  88.3 1.6 %all-to-all-done.3 = f32[64,1,128]{2,1,0:T(1,128)S(1)} async-done(((f32[64,1,128]{2,1,0:T(1,128)}), f32[64,1,128]{2,1,0:T(1,128)S(1)}, u32[]{:S(2)}, u32[]{:S(2)}) %all-to-all-start.3) | async-done | bytes 32800 | tf_op jit(solution)/shard_map/sum_scalars/all_to_all | solution.py:133
  89.9 0.1 add_divide_fusion
  90.0 0.0 copy-start.2
  90.0 0.7 copy-done.2
  90.7 0.7 multiply_add_fusion
  (18 shorter events, 0.2 us)
Async XLA Ops:
  0.6 0.8 copy-start.1
  0.6 0.8 copy-start
  1.4 29.2 %collective-permute-start = (f32[16,128]{1,0:T(8,128)S(1)}, f32[16,128]{1,0:T(8,128)S(1)}, u32[]{:S(2)}, u32[]{:S(2)}) collective-permute-start(f32[16,128]{1,0:T(8,128)S(1)} %pad_maximum_fusion.1), channel_id=1, source_target_pairs={{0,96},{1,97},{2,98},{3,99},{4,100},{5,101},{6,102},{7,103},{8,104... | collective-permute-start | bytes 24584 | tf_op jit(solution)/shard_map/gather_out_points/ppermute | solution.py:137
  6.7 24.0 %collective-permute-start.1 = (f32[16,128]{1,0:T(8,128)S(1)}, f32[16,128]{1,0:T(8,128)S(1)}, u32[]{:S(2)}, u32[]{:S(2)}) collective-permute-start(f32[16,128]{1,0:T(8,128)S(1)} %pad_maximum_fusion.1), channel_id=1, source_target_pairs={{0,64},{1,65},{2,66},{3,67},{4,68},{5,69},{6,70},{7,71},{8,72},{9,... | collective-permute-start | bytes 24584 | tf_op jit(solution)/shard_map/gather_out_points/ppermute | solution.py:137
  9.1 21.6 %collective-permute-start.2 = (f32[16,128]{1,0:T(8,128)S(1)}, f32[16,128]{1,0:T(8,128)S(1)}, u32[]{:S(2)}, u32[]{:S(2)}) collective-permute-start(f32[16,128]{1,0:T(8,128)S(1)} %pad_maximum_fusion.1), channel_id=1, source_target_pairs={{0,32},{1,33},{2,34},{3,35},{4,36},{5,37},{6,38},{7,39},{8,40},{9,... | collective-permute-start | bytes 24584 | tf_op jit(solution)/shard_map/gather_out_points/ppermute | solution.py:137
  12.3 24.0 %all-to-all-start = ((f32[16,12,128]{2,1,0:T(8,128)}), f32[16,12,128]{2,1,0:T(8,128)S(1)}, u32[]{:S(2)}, u32[]{:S(2)}) async-start(f32[16,12,128]{2,1,0:T(8,128)} %broadcast_in_dim.15), calls=%async_computation | async-start | bytes 262144 | tf_op jit(solution)/shard_map/gather_in_points_z/all_to_all | solution.py:133
  30.8 12.6 %collective-permute-start.3 = (f32[4,16,128]{2,1,0:T(8,128)S(1)}, f32[4,16,128]{2,1,0:T(8,128)S(1)}, u32[]{:S(2)}, u32[]{:S(2)}) collective-permute-start(f32[4,16,128]{2,1,0:T(8,128)S(1)} %constant_dynamic-slice_fusion), channel_id=1, source_target_pairs={{0,1},{1,0},{2,3},{3,2},{4,5},{5,4},{6,7},{7,6},{8,9},{9,8},{10,11... | collective-permute-start | bytes 98312 | tf_op jit(solution)/shard_map/gather_out_points/ppermute | solution.py:143
  37.1 10.9 %all-to-all-start.1 = ((f32[4,16,12,128]{3,1,2,0:T(8,128)}), f32[4,16,12,128]{3,1,2,0:T(8,128)S(1)}, u32[]{:S(2)}, u32[]{:S(2)}) async-start(f32[4,16,12,128]{3,1,2,0:T(8,128)} %broadcast_in_dim.16), calls=%async_computation.1 | async-start | bytes 786432 | tf_op jit(solution)/shard_map/gather_in_points_y/all_to_all | solution.py:133
  62.4 10.0 %all-to-all-start.2 = ((f32[8,8,4,128]{3,1,2,0:T(8,128)}), f32[8,8,4,128]{3,1,2,0:T(8,128)S(1)}, u32[]{:S(2)}, u32[]{:S(2)}) async-start(f32[8,8,4,128]{3,1,2,0:T(8,128)} %broadcast_in_dim.19), calls=%async_computation.2 | async-start | bytes 262144 | tf_op jit(solution)/shard_map/sum_partial_images/all_to_all | solution.py:133
  73.2 16.6 %all-to-all-start.3 = ((f32[64,1,128]{2,1,0:T(1,128)}), f32[64,1,128]{2,1,0:T(1,128)S(1)}, u32[]{:S(2)}, u32[]{:S(2)}) async-start(f32[64,1,128]{2,1,0:T(1,128)} %broadcast_in_dim.20), calls=%async_computation.3 | async-start | bytes 65536 | tf_op jit(solution)/shard_map/sum_scalars/all_to_all | solution.py:133
  90.0 0.7 copy-start.2

commit v3 on v1

v3 whole, which is shorter than its diff:
```python
import functools
import math

import jax
import jax.numpy as jnp
from jax import lax
from jax.experimental import pallas as pl
from jax.experimental.pallas import tpu as pltpu
from jax.sharding import Mesh, PartitionSpec as P

BLK = 128
LN2 = math.log(2.0)
UNIT = math.sqrt(5.0) / LN2
HALF = 1.5 / LN2
REST = 3.0 / LN2**2 - HALF**2
FRONT = LN2**2 / 3.0 * 2.0**HALF
TINY = 1e-12
FEAT = 64
S_TILE = 256
T_STEP = 4096
T_TILE = 256


def round16(x):
    return x.astype(jnp.bfloat16).astype(jnp.float32)


def split3(x):
    first = round16(x)
    rest = x - first
    second = round16(rest)
    return first, second, round16(rest - second)


def norm_rows(pts, flip):
    parts = split3(jnp.sum(pts * pts, axis=0, keepdims=True))
    row = lax.broadcasted_iota(jnp.int32, pts.shape, 0)
    at = 3 if flip else 0
    out = jnp.where((row >= 3 - at) & (row < 6 - at), 1.0, 0.0)
    for k in range(3):
        out = jnp.where(row == at + k, parts[k], out)
    return out


def out_features(pts):
    a, b, c = split3(pts)
    return jnp.concatenate([a, b, c, a, b, a, norm_rows(pts, False), jnp.zeros_like(pts)], 0)


def in_features(pts):
    a, b, c = split3(-2.0 * pts)
    return jnp.concatenate([a, a, a, b, b, c, norm_rows(pts, True), jnp.zeros_like(pts)], 0)


def prepare_kernel(own_ref, other_ref, f_ref, d_ref):
    for half, ref in enumerate((own_ref, other_ref)):
        for k in range(16):
            at = slice((half * 16 + k) * BLK, (half * 16 + k + 1) * BLK)
            rows = in_features(jnp.concatenate([ref[k, 0], ref[k, 1]], 0))
            f_ref[at, :] = jnp.transpose(rows).astype(jnp.bfloat16)
            a, b, c = split3(ref[k, 2])
            d_ref[:, at] = jnp.concatenate([a, b, c, jnp.zeros_like(a)], 0).astype(jnp.bfloat16)


def product_kernel(f_ref, d_ref, s_ref, out_ref, g_ref, acc_ref):
    n_s = s_ref.shape[0]
    for k in range(n_s):
        g_ref[:, k * BLK : (k + 1) * BLK] = out_features(s_ref[k, :8, :]).astype(jnp.bfloat16)
    acc_ref[...] = jnp.zeros_like(acc_ref)

    def step(i, carry):
        rows = pl.ds(pl.multiple_of(i * T_STEP, T_STEP), T_STEP)
        for j in range(n_s * BLK // S_TILE):
            at = slice(j * S_TILE, (j + 1) * S_TILE)
            total = acc_ref[:, at]
            for t in range(T_STEP // T_TILE):
                here = pl.ds(pl.multiple_of(i * T_STEP + t * T_TILE, T_TILE), T_TILE)
                d2 = jnp.dot(f_ref[here, :], g_ref[:, at], preferred_element_type=jnp.float32)
                d2 = jnp.maximum(d2, TINY)
                neg = -HALF - d2 * lax.rsqrt(d2)
                value = (neg * neg + REST) * jnp.exp2(neg)
                high = value.astype(jnp.bfloat16)
                low = (value - high.astype(jnp.float32)).astype(jnp.bfloat16)
                weights = d_ref[:, here]
                total = total + (
                    jnp.dot(weights, high, preferred_element_type=jnp.float32)
                    + jnp.dot(weights, low, preferred_element_type=jnp.float32)
                )
            acc_ref[:, at] = total
        return carry

    lax.fori_loop(0, f_ref.shape[0] // T_STEP, step, 0)
    total = acc_ref[0:4, :] + acc_ref[4:8, :] + acc_ref[8:12, :]
    for k in range(n_s):
        for to in range(n_s):
            out_ref[to, k, :, :] = total[:, k * BLK : (k + 1) * BLK]


def to_lanes(column):
    row = lax.broadcasted_iota(jnp.int32, (16, BLK), 0)
    lane = lax.broadcasted_iota(jnp.int32, (16, BLK), 1)
    return jnp.sum(jnp.where(row == lane, column, 0.0), axis=0, keepdims=True)


def to_column(lanes):
    row = lax.broadcasted_iota(jnp.int32, (16, BLK), 0)
    lane = lax.broadcasted_iota(jnp.int32, (16, BLK), 1)
    return jnp.sum(jnp.where(row == lane, lanes, 0.0), axis=1, keepdims=True)


def start_kernel(ls_ref, pts_ref, res_ref, dir_ref, to_yx_ref, to_z_ref, ls, pts, res, direct, sems):
    copies = [
        pltpu.make_async_copy(source, target, sems.at[k])
        for k, (source, target) in enumerate(
            ((ls_ref, ls), (pts_ref, pts), (dir_ref, direct), (res_ref, res))
        )
    ]
    for copy in copies:
        copy.start()
    for copy in copies:
        copy.wait()
    row = lax.broadcasted_iota(jnp.int32, (8, 8), 0)
    lane = lax.broadcasted_iota(jnp.int32, (8, 8), 1)
    scale = jnp.sum(jnp.where(row == lane, ls[...], 0.0), axis=1, keepdims=True)
    scaled = pts[...] / scale * UNIT
    direction, residual = direct[...], res[...]
    for k in range(16):
        to_yx_ref[k, 0:8, :] = scaled
        to_yx_ref[k, 8:12, :] = direction
        to_yx_ref[k, 12:16, :] = residual
        to_z_ref[k, 0] = scaled[0:4]
        to_z_ref[k, 1] = scaled[4:8]
        to_z_ref[k, 2] = direction


def sums_kernel(at_ref, sv_ref, nv_ref, parts_ref, s_ref, own_ref, out_ref, image_ref):
    front, noise = sv_ref[0] * FRONT, nv_ref[0]
    rr, curv, cross, square = (jnp.zeros((4, BLK), jnp.float32) for _ in range(4))
    for k in range(16):
        applied = parts_ref[0, k]
        for source in range(1, 16):
            applied = applied + parts_ref[source, k]
        s_dir, s_res = s_ref[k, 8:12, :], s_ref[k, 12:16, :]
        image = front * applied + noise * s_dir
        image_ref[k] = image
        rr, curv = rr + s_res * s_res, curv + s_dir * image
        cross, square = cross + s_res * image, square + image * image
    own_ref[...] = image_ref[at_ref[0]]
    column = jnp.sum(jnp.concatenate([rr, curv, cross, square], 0), axis=1, keepdims=True)
    lanes = to_lanes(column)
    for to in range(32):
        out_ref[to] = lanes


def end_kernel(sums_ref, own_ref, sol_ref, res_ref, dir_ref, new_sol_ref, new_res_ref, new_dir_ref):
    total = sums_ref[0]
    for k in range(1, 32):
        total = total + sums_ref[k]
    column = to_column(total)
    old_rr, curv, cross, square = (column[4 * k : 4 * k + 4] for k in range(4))
    alpha = old_rr / curv
    new_rr = old_rr - 2.0 * alpha * cross + alpha * alpha * square
    direction = dir_ref[...]
    new_residual = res_ref[...] - alpha * own_ref[...]
    new_sol_ref[...] = sol_ref[...] + alpha * direction
    new_res_ref[...] = new_residual
    new_dir_ref[...] = new_residual + (new_rr / old_rr) * direction


def call(body, shapes, where, scratch=(), entries=0, limit=40):
    spec = {
        "s": pl.BlockSpec(memory_space=pltpu.SMEM),
        "v": pl.BlockSpec(memory_space=pltpu.VMEM),
        "a": pl.BlockSpec(memory_space=pl.ANY),
    }
    return pl.pallas_call(
        body,
        out_shape=[jax.ShapeDtypeStruct(s, t) for s, t in shapes],
        in_specs=[spec[w] for w in where],
        out_specs=[pl.BlockSpec(memory_space=pltpu.VMEM) for _ in shapes],
        scratch_shapes=[x if hasattr(x, "dtype") else pltpu.VMEM(*x) for x in scratch],
        compiler_params=pltpu.CompilerParams(vmem_limit_bytes=limit * 1024 * 1024),
        cost_estimate=pl.CostEstimate(
            flops=entries * 192, bytes_accessed=0, transcendentals=entries * 2
        ),
    )


AXIS = "d"
YS, XS, ZS, CS = (2, 3, 0, 1), (2, 3, 0, 1), tuple((8 + k) % 16 for k in range(16)), (0, 1)


def flat(y, x, z, c):
    return ((y * 4 + x) * 16 + z) * 2 + c


ALONG_Z = [[flat(y, x, z, c) for z in ZS] for y in YS for x in XS for c in CS]
ALONG_YX = [[flat(y, x, z, c) for y in YS for x in XS] for z in ZS for c in CS]
ALONG_ZC = [[flat(y, x, z, c) for z in ZS for c in CS] for y in YS for x in XS]


def share(x, groups):
    return lax.all_to_all(x, AXIS, 0, 0, axis_index_groups=groups)


def on_device(points, lengthscale, signal_var, noise_var, solution, residual, direction):
    f32, bf16 = jnp.float32, jnp.bfloat16
    here = lax.axis_index(AXIS)
    place = ((here // 128 + 2) % 4 * 4 + (here // 32 + 2) % 4)[None]
    to_yx, to_z = call(
        start_kernel,
        [((16, 16, BLK), f32), ((16, 3, 4, BLK), f32)],
        "aaaa",
        [((1, 8), f32), ((8, BLK), f32), ((4, BLK), f32), ((4, BLK), f32), pltpu.SemaphoreType.DMA((4,))],
        limit=60,
    )(lengthscale[None], points, residual, direction)
    with jax.named_scope("gather_in_points"):
        t_own = share(to_z, ALONG_Z)
        t_other = lax.ppermute(t_own, AXIS, [(i, i ^ 1) for i in range(512)])
    with jax.named_scope("gather_out_points"):
        s_blocks = share(to_yx, ALONG_YX)
    n_t, n_s = 32 * BLK, 16 * BLK
    rows, weights = call(
        prepare_kernel, [((n_t, FEAT), bf16), ((16, n_t), bf16)], "vv", entries=n_t * 256
    )(t_own, t_other)
    (parts,) = call(
        product_kernel,
        [((16, 16, 4, BLK), f32)],
        "vvv",
        [((FEAT, n_s), bf16), ((16, n_s), f32)],
        n_t * n_s,
    )(rows, weights, s_blocks)
    with jax.named_scope("sum_partial_images"):
        parts = share(parts, ALONG_YX)
    own, to_zc = call(
        sums_kernel, [((4, BLK), f32), ((32, 1, BLK), f32)], "sssvv", [((16, 4, BLK), f32)]
    )(place, signal_var, noise_var, parts, s_blocks)
    with jax.named_scope("sum_scalars"):
        sums = share(to_zc, ALONG_ZC)
    return tuple(
        call(end_kernel, [((4, BLK), f32)] * 3, "vvvvv")(sums, own, solution, residual, direction)
    )


def solution(mesh):
    line = Mesh(mesh.devices.reshape(-1), (AXIS,))
    cut = P(None, AXIS)
    return jax.shard_map(
        on_device,
        mesh=line,
        in_specs=(cut, P(), P(), P(), cut, cut, cut),
        out_specs=(cut, cut, cut),
        check_vma=False,
    )
```

time: 112 us -> 84.8 us (0.76)
  waiting for transfers between devices: 27.8 us -> 6.87 us
  blocking collectives: 27.5 us -> 38.5 us
  Pallas kernels: 27.6 us -> 18.1 us
  starting transfers between devices: 22 us -> 18.8 us
  local copies, waits for them, and re-layouts: 2.81 us -> 0.01 us
  other arithmetic: 1.85 us -> 0 us
    all_to_all x3 -> x2, waiting for transfers between devices: 27.8 us -> 5.95 us  [share(): return lax.all_to_all(x, AXIS, 0, 0, axis_index_groups=groups)]
    all_to_all x1 -> x2, blocking collectives: 27.5 us -> 38.5 us  [share(): return lax.all_to_all(x, AXIS, 0, 0, axis_index_groups=groups)]
    pallas_call x1 -> x5, Pallas kernels: 27.6 us -> 18.1 us  [the longest x1 15.3 us: on_device(): call(product_kernel, [((16, 16, 4, BLK), f32)], 'vvv', [((FEAT, n_s), bf1...]
    ppermute x1, starting transfers between devices: 5.55 us -> 3.39 us  [on_device(): t_other = lax.ppermute(t_own, AXIS, [(i, i ^ 1) for i in range(512)])]
    broadcast_in_dim x4 -> x0, local copies, waits for them, and re-layouts: 2.11 us -> none  [tiled(): return jnp.broadcast_to(x[None], (n,) + x.shape)]
    all_to_all x3 -> x2, starting transfers between devices: 16.5 us -> 15.4 us  [share(): return lax.all_to_all(x, AXIS, 0, 0, axis_index_groups=groups)]
  transfers between devices with their start and end apart: 4 -> 3, of which waited for: 3 -> 2; matrix products, arithmetic and copies ran while one was open for 1% -> 0% of each run, Pallas kernels for 0% -> 0%
where the time goes in v3:
time: 84.8 us; the launch traced here: 84.3 us
  blocking collectives  38.5 us (45%)
  starting transfers between devices  18.8 us (22%)
  Pallas kernels  18.1 us (21%)
  waiting for transfers between devices  6.87 us (8%)
  between operations  1.98 us (2%)
    all_to_all x2, blocking collectives, share(): return lax.all_to_all(x, AXIS, 0, 0, axis_index_groups=groups)  38.5 us
    all_to_all x2, starting transfers between devices, share(): return lax.all_to_all(x, AXIS, 0, 0, axis_index_groups=groups)  15.4 us
    pallas_call x1, Pallas kernels, on_device(): call(product_kernel, [((16, 16, 4, BLK), f32)], 'vvv', [((FEAT, n_s), bf1...  15.3 us
    all_to_all x2, waiting for transfers between devices, share(): return lax.all_to_all(x, AXIS, 0, 0, axis_index_groups=groups)  5.95 us
    ppermute x1, starting transfers between devices, on_device(): t_other = lax.ppermute(t_own, AXIS, [(i, i ^ 1) for i in range(512)])  3.39 us
  transfers between devices with their start and end apart: 3, of which 2 were waited for; matrix products, arithmetic and copies ran while one was open for 0% of the time, Pallas kernels for 0%

profile of v3, /device:TPU:1, one launch (start us, length us, event | category | flops | bytes accessed | tf_op | source)
XLA Modules:
  0.0 84.3 jit_solution(6525782613451984345)
XLA Ops:
  0.6 1.5 %shard_map.94 = (f32[16,16,128]{2,1,0:T(8,128)}, f32[16,3,4,128]{3,2,1,0:T(4,128)}) custom-call(f32[1,8]{1,0:T(1,128)} %bitcast.2, f32[8,128]{1,0:T(8,128)} %pts_ref.1, f32[4,128]{1,0:T(4,128)} %res_ref.3, f32[4,128]{1,0:T(4,128)} %dir_ref.3), custom_call_target="tpu_custom_call" | custom-call | tf_op jit(solution)/shard_map/pallas_call | solution.py:210
  2.2 24.3 %all_to_all.20.own_ref = f32[16,3,4,128]{3,2,1,0:T(4,128)S(1)} all-to-all(f32[16,3,4,128]{3,2,1,0:T(4,128)} %get-tuple-element.9), channel_id=1, replica_groups={{336,338,340,342,344,346,348,350,320,322,324,326,328,330,332,334},{337,..., dimensions={0} | all-to-all | bytes 196608 | tf_op jit(solution)/shard_map/gather_in_points/all_to_all | solution.py:203
  26.4 8.7 %all-to-all-start.1 = ((f32[16,16,128]{2,1,0:T(8,128)}), f32[16,16,128]{2,1,0:T(8,128)S(1)}, u32[]{:S(2)}, u32[]{:S(2)}) async-start(f32[16,16,128]{2,1,0:T(8,128)} %get-tuple-element.12), calls=%async_computation.1 | async-start | bytes 262144 | tf_op jit(solution)/shard_map/gather_out_points/all_to_all | solution.py:203
  35.2 3.4 %collective-permute-start = (f32[16,3,4,128]{3,2,1,0:T(4,128)S(1)}, f32[16,3,4,128]{3,2,1,0:T(4,128)S(1)}, u32[]{:S(2)}, u32[]{:S(2)}) collective-permute-start(f32[16,3,4,128]{3,2,1,0:T(4,128)S(1)} %all_to_all.20.own_ref), channel_id=1, source_target_pairs={{0,1},{1,0},{2,3},{3,2},{4,5},{5,4},{6,7},{7,6},{8,9},{9,8},{10,11... | collective-permute-start | bytes 294920 | tf_op jit(solution)/shard_map/gather_in_points/ppermute | solution.py:219
  38.6 0.9 %collective-permute-done.other_ref = f32[16,3,4,128]{3,2,1,0:T(4,128)S(1)} collective-permute-done((f32[16,3,4,128]{3,2,1,0:T(4,128)S(1)}, f32[16,3,4,128]{3,2,1,0:T(4,128)S(1)}, u32[]{:S(2)}, u32[]{:S(2)}) %collective-permute-start) | collective-permute-done | bytes 98336 | tf_op jit(solution)/shard_map/gather_in_points/ppermute | solution.py:219
  39.5 0.4 shard_map.95
  39.9 0.0 all-to-all-done.1.s_ref
  39.9 15.3 %shard_map.96 = f32[16,16,4,128]{3,2,1,0:T(4,128)} custom-call(bf16[4096,64]{1,0:T(8,128)(2,1)S(1)} %get-tuple-element.10.f_ref, bf16[16,4096]{1,0:T(8,128)(2,1)S(1)} %get-tuple-element.11.d_ref, f32[16,16,128]{2,1,0:T(8,128)S(1)} %all-to-all-done.1.s_ref), custom_call_target="tpu_custom_call" | custom-call | flops 1610612736 | tf_op jit(solution)/shard_map/pallas_call | solution.py:226
  55.2 6.7 %all-to-all-start.2 = ((f32[16,16,4,128]{3,2,1,0:T(4,128)}), f32[16,16,4,128]{3,2,1,0:T(4,128)S(1)}, u32[]{:S(2)}, u32[]{:S(2)}) async-start(f32[16,16,4,128]{3,2,1,0:T(4,128)} %shard_map.96), calls=%async_computation.2 | async-start | bytes 1048576 | tf_op jit(solution)/shard_map/sum_partial_images/all_to_all | solution.py:203
  63.1 5.9 %all-to-all-done.2.parts_ref = f32[16,16,4,128]{3,2,1,0:T(4,128)S(1)} async-done(((f32[16,16,4,128]{3,2,1,0:T(4,128)}), f32[16,16,4,128]{3,2,1,0:T(4,128)S(1)}, u32[]{:S(2)}, u32[]{:S(2)}) %all-to-all-start.2) | async-done | bytes 524320 | tf_op jit(solution)/shard_map/sum_partial_images/all_to_all | solution.py:203
  69.1 0.0 copy-start
  69.1 0.0 copy-start.1
  69.1 0.0 copy-start.2
  69.1 0.2 shard_map.97
  69.3 14.3 %all_to_all.21.sums_ref = f32[32,1,128]{2,1,0:T(1,128)S(1)} all-to-all(f32[32,1,128]{2,1,0:T(1,128)S(1)} %get-tuple-element.13), channel_id=1, replica_groups={{336,337,338,339,340,341,342,343,344,345,346,347,348,349,350,351,320,32..., dimensions={0} | all-to-all | bytes 32768 | tf_op jit(solution)/shard_map/sum_scalars/all_to_all | solution.py:203
  83.6 0.0 copy-done
  83.6 0.0 copy-done.1
  83.6 0.0 copy-done.2
  83.6 0.8 shard_map.98
Async XLA Ops:
  26.4 13.4 %all-to-all-start.1 = ((f32[16,16,128]{2,1,0:T(8,128)}), f32[16,16,128]{2,1,0:T(8,128)S(1)}, u32[]{:S(2)}, u32[]{:S(2)}) async-start(f32[16,16,128]{2,1,0:T(8,128)} %get-tuple-element.12), calls=%async_computation.1 | async-start | bytes 262144 | tf_op jit(solution)/shard_map/gather_out_points/all_to_all | solution.py:203
  35.2 4.3 %collective-permute-start = (f32[16,3,4,128]{3,2,1,0:T(4,128)S(1)}, f32[16,3,4,128]{3,2,1,0:T(4,128)S(1)}, u32[]{:S(2)}, u32[]{:S(2)}) collective-permute-start(f32[16,3,4,128]{3,2,1,0:T(4,128)S(1)} %all_to_all.20.own_ref), channel_id=1, source_target_pairs={{0,1},{1,0},{2,3},{3,2},{4,5},{5,4},{6,7},{7,6},{8,9},{9,8},{10,11... | collective-permute-start | bytes 294920 | tf_op jit(solution)/shard_map/gather_in_points/ppermute | solution.py:219
  55.2 13.9 %all-to-all-start.2 = ((f32[16,16,4,128]{3,2,1,0:T(4,128)}), f32[16,16,4,128]{3,2,1,0:T(4,128)S(1)}, u32[]{:S(2)}, u32[]{:S(2)}) async-start(f32[16,16,4,128]{3,2,1,0:T(4,128)} %shard_map.96), calls=%async_computation.2 | async-start | bytes 1048576 | tf_op jit(solution)/shard_map/sum_partial_images/all_to_all | solution.py:203
  69.1 14.5 %copy-start = (f32[4,128]{1,0:T(4,128)S(1)}, f32[4,128]{1,0:T(4,128)}, u32[]{:S(2)}) copy-start(f32[4,128]{1,0:T(4,128)} %res_ref.3) | copy-start | bytes 6148
  69.1 14.5 %copy-start.1 = (f32[4,128]{1,0:T(4,128)S(1)}, f32[4,128]{1,0:T(4,128)}, u32[]{:S(2)}) copy-start(f32[4,128]{1,0:T(4,128)} %dir_ref.3) | copy-start | bytes 6148
  69.1 14.5 %copy-start.2 = (f32[4,128]{1,0:T(4,128)S(1)}, f32[4,128]{1,0:T(4,128)}, u32[]{:S(2)}) copy-start(f32[4,128]{1,0:T(4,128)} %sol_ref.1) | copy-start | bytes 6148

commit v4 on v3

--- a/solution.py
+++ b/solution.py
@@ -14,7 +14,6 @@
 HALF = 1.5 / LN2
 REST = 3.0 / LN2**2 - HALF**2
 FRONT = LN2**2 / 3.0 * 2.0**HALF
-TINY = 1e-12
 FEAT = 64
 S_TILE = 256
 T_STEP = 4096
@@ -76,8 +75,7 @@
             for t in range(T_STEP // T_TILE):
                 here = pl.ds(pl.multiple_of(i * T_STEP + t * T_TILE, T_TILE), T_TILE)
                 d2 = jnp.dot(f_ref[here, :], g_ref[:, at], preferred_element_type=jnp.float32)
-                d2 = jnp.maximum(d2, TINY)
-                neg = -HALF - d2 * lax.rsqrt(d2)
+                neg = -HALF - lax.rsqrt(lax.rsqrt(d2 * d2))
                 value = (neg * neg + REST) * jnp.exp2(neg)
                 high = value.astype(jnp.bfloat16)
                 low = (value - high.astype(jnp.float32)).astype(jnp.bfloat16)

time: 84.8 us -> 83.9 us (0.989)
    pallas_call x1, Pallas kernels: 15.3 us -> 14.4 us  [on_device(): call(product_kernel, [((16, 16, 4, BLK), f32)], 'vvv', [((FEAT, n_s), bf1...]
where the time goes in v4:
time: 83.9 us; the launch traced here: 83.5 us
  blocking collectives  38.5 us (46%)
  starting transfers between devices  18.8 us (22%)
  Pallas kernels  17.3 us (21%)
  waiting for transfers between devices  6.87 us (8%)
  between operations  1.98 us (2%)
    all_to_all x2, blocking collectives, share(): return lax.all_to_all(x, AXIS, 0, 0, axis_index_groups=groups)  38.5 us
    all_to_all x2, starting transfers between devices, share(): return lax.all_to_all(x, AXIS, 0, 0, axis_index_groups=groups)  15.4 us
    pallas_call x1, Pallas kernels, on_device(): call(product_kernel, [((16, 16, 4, BLK), f32)], 'vvv', [((FEAT, n_s), bf1...  14.4 us
    all_to_all x2, waiting for transfers between devices, share(): return lax.all_to_all(x, AXIS, 0, 0, axis_index_groups=groups)  5.95 us
    ppermute x1, starting transfers between devices, on_device(): t_other = lax.ppermute(t_own, AXIS, [(i, i ^ 1) for i in range(512)])  3.39 us
  transfers between devices with their start and end apart: 3, of which 2 were waited for; matrix products, arithmetic and copies ran while one was open for 0% of the time, Pallas kernels for 0%

profile of v4, /device:TPU:1, one launch (start us, length us, event | category | flops | bytes accessed | tf_op | source)
XLA Modules:
  0.0 83.5 jit_solution(13141616039627035418)
XLA Ops:
  0.6 1.5 %shard_map.94 = (f32[16,16,128]{2,1,0:T(8,128)}, f32[16,3,4,128]{3,2,1,0:T(4,128)}) custom-call(f32[1,8]{1,0:T(1,128)} %bitcast.2, f32[8,128]{1,0:T(8,128)} %pts_ref.1, f32[4,128]{1,0:T(4,128)} %res_ref.3, f32[4,128]{1,0:T(4,128)} %dir_ref.3), custom_call_target="tpu_custom_call" | custom-call | tf_op jit(solution)/shard_map/pallas_call | solution.py:208
  2.2 24.3 %all_to_all.20.own_ref = f32[16,3,4,128]{3,2,1,0:T(4,128)S(1)} all-to-all(f32[16,3,4,128]{3,2,1,0:T(4,128)} %get-tuple-element.9), channel_id=1, replica_groups={{336,338,340,342,344,346,348,350,320,322,324,326,328,330,332,334},{337,..., dimensions={0} | all-to-all | bytes 196608 | tf_op jit(solution)/shard_map/gather_in_points/all_to_all | solution.py:201
  26.4 8.7 %all-to-all-start.1 = ((f32[16,16,128]{2,1,0:T(8,128)}), f32[16,16,128]{2,1,0:T(8,128)S(1)}, u32[]{:S(2)}, u32[]{:S(2)}) async-start(f32[16,16,128]{2,1,0:T(8,128)} %get-tuple-element.12), calls=%async_computation.1 | async-start | bytes 262144 | tf_op jit(solution)/shard_map/gather_out_points/all_to_all | solution.py:201
  35.2 3.4 %collective-permute-start = (f32[16,3,4,128]{3,2,1,0:T(4,128)S(1)}, f32[16,3,4,128]{3,2,1,0:T(4,128)S(1)}, u32[]{:S(2)}, u32[]{:S(2)}) collective-permute-start(f32[16,3,4,128]{3,2,1,0:T(4,128)S(1)} %all_to_all.20.own_ref), channel_id=1, source_target_pairs={{0,1},{1,0},{2,3},{3,2},{4,5},{5,4},{6,7},{7,6},{8,9},{9,8},{10,11... | collective-permute-start | bytes 294920 | tf_op jit(solution)/shard_map/gather_in_points/ppermute | solution.py:217
  38.6 0.9 %collective-permute-done.other_ref = f32[16,3,4,128]{3,2,1,0:T(4,128)S(1)} collective-permute-done((f32[16,3,4,128]{3,2,1,0:T(4,128)S(1)}, f32[16,3,4,128]{3,2,1,0:T(4,128)S(1)}, u32[]{:S(2)}, u32[]{:S(2)}) %collective-permute-start) | collective-permute-done | bytes 98336 | tf_op jit(solution)/shard_map/gather_in_points/ppermute | solution.py:217
  39.5 0.4 shard_map.95
  39.9 0.0 all-to-all-done.1.s_ref
  39.9 14.4 %shard_map.96 = f32[16,16,4,128]{3,2,1,0:T(4,128)} custom-call(bf16[4096,64]{1,0:T(8,128)(2,1)S(1)} %get-tuple-element.10.f_ref, bf16[16,4096]{1,0:T(8,128)(2,1)S(1)} %get-tuple-element.11.d_ref, f32[16,16,128]{2,1,0:T(8,128)S(1)} %all-to-all-done.1.s_ref), custom_call_target="tpu_custom_call" | custom-call | flops 1610612736 | tf_op jit(solution)/shard_map/pallas_call | solution.py:224
  54.3 6.7 %all-to-all-start.2 = ((f32[16,16,4,128]{3,2,1,0:T(4,128)}), f32[16,16,4,128]{3,2,1,0:T(4,128)S(1)}, u32[]{:S(2)}, u32[]{:S(2)}) async-start(f32[16,16,4,128]{3,2,1,0:T(4,128)} %shard_map.96), calls=%async_computation.2 | async-start | bytes 1048576 | tf_op jit(solution)/shard_map/sum_partial_images/all_to_all | solution.py:201
  62.3 5.9 %all-to-all-done.2.parts_ref = f32[16,16,4,128]{3,2,1,0:T(4,128)S(1)} async-done(((f32[16,16,4,128]{3,2,1,0:T(4,128)}), f32[16,16,4,128]{3,2,1,0:T(4,128)S(1)}, u32[]{:S(2)}, u32[]{:S(2)}) %all-to-all-start.2) | async-done | bytes 524320 | tf_op jit(solution)/shard_map/sum_partial_images/all_to_all | solution.py:201
  68.2 0.0 copy-start
  68.2 0.0 copy-start.1
  68.2 0.0 copy-start.2
  68.2 0.2 shard_map.97
  68.4 14.3 %all_to_all.21.sums_ref = f32[32,1,128]{2,1,0:T(1,128)S(1)} all-to-all(f32[32,1,128]{2,1,0:T(1,128)S(1)} %get-tuple-element.13), channel_id=1, replica_groups={{336,337,338,339,340,341,342,343,344,345,346,347,348,349,350,351,320,32..., dimensions={0} | all-to-all | bytes 32768 | tf_op jit(solution)/shard_map/sum_scalars/all_to_all | solution.py:201
  82.7 0.0 copy-done
  82.7 0.0 copy-done.1
  82.7 0.0 copy-done.2
  82.7 0.8 shard_map.98
Async XLA Ops:
  26.4 13.4 %all-to-all-start.1 = ((f32[16,16,128]{2,1,0:T(8,128)}), f32[16,16,128]{2,1,0:T(8,128)S(1)}, u32[]{:S(2)}, u32[]{:S(2)}) async-start(f32[16,16,128]{2,1,0:T(8,128)} %get-tuple-element.12), calls=%async_computation.1 | async-start | bytes 262144 | tf_op jit(solution)/shard_map/gather_out_points/all_to_all | solution.py:201
  35.2 4.3 %collective-permute-start = (f32[16,3,4,128]{3,2,1,0:T(4,128)S(1)}, f32[16,3,4,128]{3,2,1,0:T(4,128)S(1)}, u32[]{:S(2)}, u32[]{:S(2)}) collective-permute-start(f32[16,3,4,128]{3,2,1,0:T(4,128)S(1)} %all_to_all.20.own_ref), channel_id=1, source_target_pairs={{0,1},{1,0},{2,3},{3,2},{4,5},{5,4},{6,7},{7,6},{8,9},{9,8},{10,11... | collective-permute-start | bytes 294920 | tf_op jit(solution)/shard_map/gather_in_points/ppermute | solution.py:217
  54.3 13.9 %all-to-all-start.2 = ((f32[16,16,4,128]{3,2,1,0:T(4,128)}), f32[16,16,4,128]{3,2,1,0:T(4,128)S(1)}, u32[]{:S(2)}, u32[]{:S(2)}) async-start(f32[16,16,4,128]{3,2,1,0:T(4,128)} %shard_map.96), calls=%async_computation.2 | async-start | bytes 1048576 | tf_op jit(solution)/shard_map/sum_partial_images/all_to_all | solution.py:201
  68.2 14.5 %copy-start = (f32[4,128]{1,0:T(4,128)S(1)}, f32[4,128]{1,0:T(4,128)}, u32[]{:S(2)}) copy-start(f32[4,128]{1,0:T(4,128)} %res_ref.3) | copy-start | bytes 6148
  68.2 14.5 %copy-start.1 = (f32[4,128]{1,0:T(4,128)S(1)}, f32[4,128]{1,0:T(4,128)}, u32[]{:S(2)}) copy-start(f32[4,128]{1,0:T(4,128)} %dir_ref.3) | copy-start | bytes 6148
  68.2 14.5 %copy-start.2 = (f32[4,128]{1,0:T(4,128)S(1)}, f32[4,128]{1,0:T(4,128)}, u32[]{:S(2)}) copy-start(f32[4,128]{1,0:T(4,128)} %sol_ref.1) | copy-start | bytes 6148

commit v5 on v4

--- a/solution.py
+++ b/solution.py
@@ -173,7 +173,7 @@
     }
     return pl.pallas_call(
         body,
-        out_shape=[jax.ShapeDtypeStruct(s, t) for s, t in shapes],
+        out_shape=[x if hasattr(x, "memory_space") else jax.ShapeDtypeStruct(*x) for x in shapes],
         in_specs=[spec[w] for w in where],
         out_specs=[pl.BlockSpec(memory_space=pltpu.VMEM) for _ in shapes],
         scratch_shapes=[x if hasattr(x, "dtype") else pltpu.VMEM(*x) for x in scratch],
@@ -194,6 +194,7 @@
 
 ALONG_Z = [[flat(y, x, z, c) for z in ZS] for y in YS for x in XS for c in CS]
 ALONG_YX = [[flat(y, x, z, c) for y in YS for x in XS] for z in ZS for c in CS]
+DIAGONAL_YX = [[flat((2 + k) % 4, (2 + k // 4 + k) % 4, z, c) for k in range(16)] for z in ZS for c in CS]
 ALONG_ZC = [[flat(y, x, z, c) for z in ZS for c in CS] for y in YS for x in XS]
 
 
@@ -207,7 +208,7 @@
     place = ((here // 128 + 2) % 4 * 4 + (here // 32 + 2) % 4)[None]
     to_yx, to_z = call(
         start_kernel,
-        [((16, 16, BLK), f32), ((16, 3, 4, BLK), f32)],
+        [pltpu.VMEM((16, 16, BLK), f32), pltpu.VMEM((16, 3, 4, BLK), f32)],
         "aaaa",
         [((1, 8), f32), ((8, BLK), f32), ((4, BLK), f32), ((4, BLK), f32), pltpu.SemaphoreType.DMA((4,))],
         limit=60,
@@ -219,19 +220,19 @@
         s_blocks = share(to_yx, ALONG_YX)
     n_t, n_s = 32 * BLK, 16 * BLK
     rows, weights = call(
-        prepare_kernel, [((n_t, FEAT), bf16), ((16, n_t), bf16)], "vv", entries=n_t * 256
+        prepare_kernel, [pltpu.VMEM((n_t, FEAT), bf16), pltpu.VMEM((16, n_t), bf16)], "vv", entries=n_t * 256
     )(t_own, t_other)
     (parts,) = call(
         product_kernel,
-        [((16, 16, 4, BLK), f32)],
+        [pltpu.VMEM((16, 16, 4, BLK), f32)],
         "vvv",
         [((FEAT, n_s), bf16), ((16, n_s), f32)],
         n_t * n_s,
     )(rows, weights, s_blocks)
     with jax.named_scope("sum_partial_images"):
-        parts = share(parts, ALONG_YX)
+        parts = share(parts, DIAGONAL_YX)
     own, to_zc = call(
-        sums_kernel, [((4, BLK), f32), ((32, 1, BLK), f32)], "sssvv", [((16, 4, BLK), f32)]
+        sums_kernel, [pltpu.VMEM((4, BLK), f32), pltpu.VMEM((32, 1, BLK), f32)], "sssvv", [((16, 4, BLK), f32)]
     )(place, signal_var, noise_var, parts, s_blocks)
     with jax.named_scope("sum_scalars"):
         sums = share(to_zc, ALONG_ZC)

time: 83.9 us -> 83.4 us (level)
  waiting for transfers between devices: 6.87 us -> 5.55 us
  blocking collectives: 38.5 us -> 39.4 us
    all_to_all x2, waiting for transfers between devices: 5.95 us -> 4.63 us  [share(): return lax.all_to_all(x, AXIS, 0, 0, axis_index_groups=groups)]
where the time goes in v5:
time: 83.4 us; the launch traced here: 82.9 us
  blocking collectives  39.4 us (47%)
  starting transfers between devices  18.8 us (23%)
  Pallas kernels  17.2 us (21%)
  waiting for transfers between devices  5.55 us (7%)
  between operations  1.98 us (2%)
    all_to_all x2, blocking collectives, share(): return lax.all_to_all(x, AXIS, 0, 0, axis_index_groups=groups)  39.4 us
    all_to_all x2, starting transfers between devices, share(): return lax.all_to_all(x, AXIS, 0, 0, axis_index_groups=groups)  15.4 us
    pallas_call x1, Pallas kernels, on_device(): call(product_kernel, [pltpu.VMEM((16, 16, 4, BLK), f32)], 'vvv', [((FEAT,...  14.4 us
    all_to_all x2, waiting for transfers between devices, share(): return lax.all_to_all(x, AXIS, 0, 0, axis_index_groups=groups)  4.63 us
    ppermute x1, starting transfers between devices, on_device(): t_other = lax.ppermute(t_own, AXIS, [(i, i ^ 1) for i in range(512)])  3.39 us
  transfers between devices with their start and end apart: 3, of which 2 were waited for; matrix products, arithmetic and copies ran while one was open for 0% of the time, Pallas kernels for 0%

profile of v5, /device:TPU:1, one launch (start us, length us, event | category | flops | bytes accessed | tf_op | source)
XLA Modules:
  0.0 82.9 jit_solution(4270054128382349098)
XLA Ops:
  0.6 1.5 %shard_map.94 = (f32[16,16,128]{2,1,0:T(8,128)}, f32[16,3,4,128]{3,2,1,0:T(4,128)S(1)}) custom-call(f32[1,8]{1,0:T(1,128)} %bitcast.2, f32[8,128]{1,0:T(8,128)} %pts_ref.1, f32[4,128]{1,0:T(4,128)} %res_ref.3, f32[4,128]{1,0:T(4,128)} %dir_ref.3), custom_call_target="tpu_custom_call" | custom-call | tf_op jit(solution)/shard_map/pallas_call | solution.py:209
  2.1 24.0 %all_to_all.20.own_ref = f32[16,3,4,128]{3,2,1,0:T(4,128)S(1)} all-to-all(f32[16,3,4,128]{3,2,1,0:T(4,128)S(1)} %get-tuple-element.9), channel_id=1, replica_groups={{336,338,340,342,344,346,348,350,320,322,324,326,328,330,332,334},{337,..., dimensions={0} | all-to-all | bytes 196608 | tf_op jit(solution)/shard_map/gather_in_points/all_to_all | solution.py:202
  26.2 8.7 %all-to-all-start.1 = ((f32[16,16,128]{2,1,0:T(8,128)}), f32[16,16,128]{2,1,0:T(8,128)S(1)}, u32[]{:S(2)}, u32[]{:S(2)}) async-start(f32[16,16,128]{2,1,0:T(8,128)} %get-tuple-element.12), calls=%async_computation.1 | async-start | bytes 262144 | tf_op jit(solution)/shard_map/gather_out_points/all_to_all | solution.py:202
  34.9 3.4 %collective-permute-start = (f32[16,3,4,128]{3,2,1,0:T(4,128)S(1)}, f32[16,3,4,128]{3,2,1,0:T(4,128)S(1)}, u32[]{:S(2)}, u32[]{:S(2)}) collective-permute-start(f32[16,3,4,128]{3,2,1,0:T(4,128)S(1)} %all_to_all.20.own_ref), channel_id=1, source_target_pairs={{0,1},{1,0},{2,3},{3,2},{4,5},{5,4},{6,7},{7,6},{8,9},{9,8},{10,11... | collective-permute-start | bytes 294920 | tf_op jit(solution)/shard_map/gather_in_points/ppermute | solution.py:218
  38.3 0.9 %collective-permute-done.other_ref = f32[16,3,4,128]{3,2,1,0:T(4,128)S(1)} collective-permute-done((f32[16,3,4,128]{3,2,1,0:T(4,128)S(1)}, f32[16,3,4,128]{3,2,1,0:T(4,128)S(1)}, u32[]{:S(2)}, u32[]{:S(2)}) %collective-permute-start) | collective-permute-done | bytes 98336 | tf_op jit(solution)/shard_map/gather_in_points/ppermute | solution.py:218
  39.2 0.4 shard_map.95
  39.6 0.0 all-to-all-done.1.s_ref
  39.6 14.4 %shard_map.96 = f32[16,16,4,128]{3,2,1,0:T(4,128)} custom-call(bf16[4096,64]{1,0:T(8,128)(2,1)S(1)} %get-tuple-element.10.f_ref, bf16[16,4096]{1,0:T(8,128)(2,1)S(1)} %get-tuple-element.11.d_ref, f32[16,16,128]{2,1,0:T(8,128)S(1)} %all-to-all-done.1.s_ref), custom_call_target="tpu_custom_call" | custom-call | flops 1610612736 | tf_op jit(solution)/shard_map/pallas_call | solution.py:225
  54.0 6.7 %all-to-all-start.2 = ((f32[16,16,4,128]{3,2,1,0:T(4,128)}), f32[16,16,4,128]{3,2,1,0:T(4,128)S(1)}, u32[]{:S(2)}, u32[]{:S(2)}) async-start(f32[16,16,4,128]{3,2,1,0:T(4,128)} %shard_map.96), calls=%async_computation.2 | async-start | bytes 1048576 | tf_op jit(solution)/shard_map/sum_partial_images/all_to_all | solution.py:202
  62.0 4.6 %all-to-all-done.2.parts_ref = f32[16,16,4,128]{3,2,1,0:T(4,128)S(1)} async-done(((f32[16,16,4,128]{3,2,1,0:T(4,128)}), f32[16,16,4,128]{3,2,1,0:T(4,128)S(1)}, u32[]{:S(2)}, u32[]{:S(2)}) %all-to-all-start.2) | async-done | bytes 524320 | tf_op jit(solution)/shard_map/sum_partial_images/all_to_all | solution.py:202
  66.6 0.0 copy-start
  66.6 0.0 copy-start.1
  66.6 0.0 copy-start.2
  66.6 0.2 shard_map.97
  66.8 15.3 %all_to_all.21.sums_ref = f32[32,1,128]{2,1,0:T(1,128)S(1)} all-to-all(f32[32,1,128]{2,1,0:T(1,128)S(1)} %get-tuple-element.13), channel_id=1, replica_groups={{336,337,338,339,340,341,342,343,344,345,346,347,348,349,350,351,320,32..., dimensions={0} | all-to-all | bytes 32768 | tf_op jit(solution)/shard_map/sum_scalars/all_to_all | solution.py:202
  82.1 0.0 copy-done
  82.1 0.0 copy-done.1
  82.1 0.0 copy-done.2
  82.1 0.8 shard_map.98
Async XLA Ops:
  26.2 13.4 %all-to-all-start.1 = ((f32[16,16,128]{2,1,0:T(8,128)}), f32[16,16,128]{2,1,0:T(8,128)S(1)}, u32[]{:S(2)}, u32[]{:S(2)}) async-start(f32[16,16,128]{2,1,0:T(8,128)} %get-tuple-element.12), calls=%async_computation.1 | async-start | bytes 262144 | tf_op jit(solution)/shard_map/gather_out_points/all_to_all | solution.py:202
  34.9 4.3 %collective-permute-start = (f32[16,3,4,128]{3,2,1,0:T(4,128)S(1)}, f32[16,3,4,128]{3,2,1,0:T(4,128)S(1)}, u32[]{:S(2)}, u32[]{:S(2)}) collective-permute-start(f32[16,3,4,128]{3,2,1,0:T(4,128)S(1)} %all_to_all.20.own_ref), channel_id=1, source_target_pairs={{0,1},{1,0},{2,3},{3,2},{4,5},{5,4},{6,7},{7,6},{8,9},{9,8},{10,11... | collective-permute-start | bytes 294920 | tf_op jit(solution)/shard_map/gather_in_points/ppermute | solution.py:218
  54.0 12.6 %all-to-all-start.2 = ((f32[16,16,4,128]{3,2,1,0:T(4,128)}), f32[16,16,4,128]{3,2,1,0:T(4,128)S(1)}, u32[]{:S(2)}, u32[]{:S(2)}) async-start(f32[16,16,4,128]{3,2,1,0:T(4,128)} %shard_map.96), calls=%async_computation.2 | async-start | bytes 1048576 | tf_op jit(solution)/shard_map/sum_partial_images/all_to_all | solution.py:202
  66.6 15.5 %copy-start = (f32[4,128]{1,0:T(4,128)S(1)}, f32[4,128]{1,0:T(4,128)}, u32[]{:S(2)}) copy-start(f32[4,128]{1,0:T(4,128)} %res_ref.3) | copy-start | bytes 6148
  66.6 15.5 %copy-start.1 = (f32[4,128]{1,0:T(4,128)S(1)}, f32[4,128]{1,0:T(4,128)}, u32[]{:S(2)}) copy-start(f32[4,128]{1,0:T(4,128)} %dir_ref.3) | copy-start | bytes 6148
  66.6 15.5 %copy-start.2 = (f32[4,128]{1,0:T(4,128)S(1)}, f32[4,128]{1,0:T(4,128)}, u32[]{:S(2)}) copy-start(f32[4,128]{1,0:T(4,128)} %sol_ref.1) | copy-start | bytes 6148

commit v6 on v5

--- a/solution.py
+++ b/solution.py
@@ -17,7 +17,7 @@
 FEAT = 64
 S_TILE = 256
 T_STEP = 4096
-T_TILE = 256
+T_TILE = 128
 
 
 def round16(x):
@@ -193,7 +193,6 @@
 
 
 ALONG_Z = [[flat(y, x, z, c) for z in ZS] for y in YS for x in XS for c in CS]
-ALONG_YX = [[flat(y, x, z, c) for y in YS for x in XS] for z in ZS for c in CS]
 DIAGONAL_YX = [[flat((2 + k) % 4, (2 + k // 4 + k) % 4, z, c) for k in range(16)] for z in ZS for c in CS]
 ALONG_ZC = [[flat(y, x, z, c) for z in ZS for c in CS] for y in YS for x in XS]
 
@@ -205,7 +204,8 @@
 def on_device(points, lengthscale, signal_var, noise_var, solution, residual, direction):
     f32, bf16 = jnp.float32, jnp.bfloat16
     here = lax.axis_index(AXIS)
-    place = ((here // 128 + 2) % 4 * 4 + (here // 32 + 2) % 4)[None]
+    from_y = (here // 128 + 2) % 4
+    place = ((here // 32 + 2 - from_y) % 4 * 4 + from_y)[None]
     to_yx, to_z = call(
         start_kernel,
         [pltpu.VMEM((16, 16, BLK), f32), pltpu.VMEM((16, 3, 4, BLK), f32)],
@@ -217,7 +217,7 @@
         t_own = share(to_z, ALONG_Z)
         t_other = lax.ppermute(t_own, AXIS, [(i, i ^ 1) for i in range(512)])
     with jax.named_scope("gather_out_points"):
-        s_blocks = share(to_yx, ALONG_YX)
+        s_blocks = share(to_yx, DIAGONAL_YX)
     n_t, n_s = 32 * BLK, 16 * BLK
     rows, weights = call(
         prepare_kernel, [pltpu.VMEM((n_t, FEAT), bf16), pltpu.VMEM((16, n_t), bf16)], "vv", entries=n_t * 256

time: 83.4 us -> 83.3 us (level)
  no operation moved by 1% of the time
where the time goes in v6:
time: 83.3 us; the launch traced here: 82.8 us
  blocking collectives  39.9 us (48%)
  starting transfers between devices  18.7 us (22%)
  Pallas kernels  17.1 us (21%)
  waiting for transfers between devices  5.05 us (6%)
  between operations  1.97 us (2%)
    all_to_all x2, blocking collectives, share(): return lax.all_to_all(x, AXIS, 0, 0, axis_index_groups=groups)  39.9 us
    all_to_all x2, starting transfers between devices, share(): return lax.all_to_all(x, AXIS, 0, 0, axis_index_groups=groups)  15.3 us
    pallas_call x1, Pallas kernels, on_device(): call(product_kernel, [pltpu.VMEM((16, 16, 4, BLK), f32)], 'vvv', [((FEAT,...  14.3 us
    all_to_all x2, waiting for transfers between devices, share(): return lax.all_to_all(x, AXIS, 0, 0, axis_index_groups=groups)  4.13 us
    ppermute x1, starting transfers between devices, on_device(): t_other = lax.ppermute(t_own, AXIS, [(i, i ^ 1) for i in range(512)])  3.39 us
  transfers between devices with their start and end apart: 3, of which 2 were waited for; matrix products, arithmetic and copies ran while one was open for 0% of the time, Pallas kernels for 0%

profile of v6, /device:TPU:1, one launch (start us, length us, event | category | flops | bytes accessed | tf_op | source)
XLA Modules:
  0.0 82.8 jit_solution(11844727268566933892)
XLA Ops:
  0.6 1.5 %shard_map.94 = (f32[16,16,128]{2,1,0:T(8,128)}, f32[16,3,4,128]{3,2,1,0:T(4,128)S(1)}) custom-call(f32[1,8]{1,0:T(1,128)} %bitcast.2, f32[8,128]{1,0:T(8,128)} %pts_ref.1, f32[4,128]{1,0:T(4,128)} %res_ref.3, f32[4,128]{1,0:T(4,128)} %dir_ref.3), custom_call_target="tpu_custom_call" | custom-call | tf_op jit(solution)/shard_map/pallas_call | solution.py:209
  2.1 24.0 %all_to_all.20.own_ref = f32[16,3,4,128]{3,2,1,0:T(4,128)S(1)} all-to-all(f32[16,3,4,128]{3,2,1,0:T(4,128)S(1)} %get-tuple-element.9), channel_id=1, replica_groups={{336,338,340,342,344,346,348,350,320,322,324,326,328,330,332,334},{337,..., dimensions={0} | all-to-all | bytes 196608 | tf_op jit(solution)/shard_map/gather_in_points/all_to_all | solution.py:201
  26.2 8.7 %all-to-all-start.1 = ((f32[16,16,128]{2,1,0:T(8,128)}), f32[16,16,128]{2,1,0:T(8,128)S(1)}, u32[]{:S(2)}, u32[]{:S(2)}) async-start(f32[16,16,128]{2,1,0:T(8,128)} %get-tuple-element.12), calls=%async_computation.1 | async-start | bytes 262144 | tf_op jit(solution)/shard_map/gather_out_points/all_to_all | solution.py:201
  34.9 3.4 %collective-permute-start = (f32[16,3,4,128]{3,2,1,0:T(4,128)S(1)}, f32[16,3,4,128]{3,2,1,0:T(4,128)S(1)}, u32[]{:S(2)}, u32[]{:S(2)}) collective-permute-start(f32[16,3,4,128]{3,2,1,0:T(4,128)S(1)} %all_to_all.20.own_ref), channel_id=1, source_target_pairs={{0,1},{1,0},{2,3},{3,2},{4,5},{5,4},{6,7},{7,6},{8,9},{9,8},{10,11... | collective-permute-start | bytes 294920 | tf_op jit(solution)/shard_map/gather_in_points/ppermute | solution.py:218
  38.3 0.9 %collective-permute-done.other_ref = f32[16,3,4,128]{3,2,1,0:T(4,128)S(1)} collective-permute-done((f32[16,3,4,128]{3,2,1,0:T(4,128)S(1)}, f32[16,3,4,128]{3,2,1,0:T(4,128)S(1)}, u32[]{:S(2)}, u32[]{:S(2)}) %collective-permute-start) | collective-permute-done | bytes 98336 | tf_op jit(solution)/shard_map/gather_in_points/ppermute | solution.py:218
  39.2 0.4 shard_map.95
  39.6 0.0 all-to-all-done.1.s_ref
  39.6 14.3 %shard_map.96 = f32[16,16,4,128]{3,2,1,0:T(4,128)} custom-call(bf16[4096,64]{1,0:T(8,128)(2,1)S(1)} %get-tuple-element.10.f_ref, bf16[16,4096]{1,0:T(8,128)(2,1)S(1)} %get-tuple-element.11.d_ref, f32[16,16,128]{2,1,0:T(8,128)S(1)} %all-to-all-done.1.s_ref), custom_call_target="tpu_custom_call" | custom-call | flops 1610612736 | tf_op jit(solution)/shard_map/pallas_call | solution.py:225
  53.9 6.7 %all-to-all-start.2 = ((f32[16,16,4,128]{3,2,1,0:T(4,128)}), f32[16,16,4,128]{3,2,1,0:T(4,128)S(1)}, u32[]{:S(2)}, u32[]{:S(2)}) async-start(f32[16,16,4,128]{3,2,1,0:T(4,128)} %shard_map.96), calls=%async_computation.2 | async-start | bytes 1048576 | tf_op jit(solution)/shard_map/sum_partial_images/all_to_all | solution.py:201
  61.9 4.1 %all-to-all-done.2.parts_ref = f32[16,16,4,128]{3,2,1,0:T(4,128)S(1)} async-done(((f32[16,16,4,128]{3,2,1,0:T(4,128)}), f32[16,16,4,128]{3,2,1,0:T(4,128)S(1)}, u32[]{:S(2)}, u32[]{:S(2)}) %all-to-all-start.2) | async-done | bytes 524320 | tf_op jit(solution)/shard_map/sum_partial_images/all_to_all | solution.py:201
  66.0 0.0 copy-start
  66.0 0.0 copy-start.1
  66.0 0.0 copy-start.2
  66.0 0.2 shard_map.97
  66.2 15.9 %all_to_all.21.sums_ref = f32[32,1,128]{2,1,0:T(1,128)S(1)} all-to-all(f32[32,1,128]{2,1,0:T(1,128)S(1)} %get-tuple-element.13), channel_id=1, replica_groups={{336,337,338,339,340,341,342,343,344,345,346,347,348,349,350,351,320,32..., dimensions={0} | all-to-all | bytes 32768 | tf_op jit(solution)/shard_map/sum_scalars/all_to_all | solution.py:201
  82.0 0.0 copy-done
  82.0 0.0 copy-done.1
  82.0 0.0 copy-done.2
  82.0 0.8 shard_map.98
Async XLA Ops:
  26.2 13.4 %all-to-all-start.1 = ((f32[16,16,128]{2,1,0:T(8,128)}), f32[16,16,128]{2,1,0:T(8,128)S(1)}, u32[]{:S(2)}, u32[]{:S(2)}) async-start(f32[16,16,128]{2,1,0:T(8,128)} %get-tuple-element.12), calls=%async_computation.1 | async-start | bytes 262144 | tf_op jit(solution)/shard_map/gather_out_points/all_to_all | solution.py:201
  34.9 4.3 %collective-permute-start = (f32[16,3,4,128]{3,2,1,0:T(4,128)S(1)}, f32[16,3,4,128]{3,2,1,0:T(4,128)S(1)}, u32[]{:S(2)}, u32[]{:S(2)}) collective-permute-start(f32[16,3,4,128]{3,2,1,0:T(4,128)S(1)} %all_to_all.20.own_ref), channel_id=1, source_target_pairs={{0,1},{1,0},{2,3},{3,2},{4,5},{5,4},{6,7},{7,6},{8,9},{9,8},{10,11... | collective-permute-start | bytes 294920 | tf_op jit(solution)/shard_map/gather_in_points/ppermute | solution.py:218
  53.9 12.1 %all-to-all-start.2 = ((f32[16,16,4,128]{3,2,1,0:T(4,128)}), f32[16,16,4,128]{3,2,1,0:T(4,128)S(1)}, u32[]{:S(2)}, u32[]{:S(2)}) async-start(f32[16,16,4,128]{3,2,1,0:T(4,128)} %shard_map.96), calls=%async_computation.2 | async-start | bytes 1048576 | tf_op jit(solution)/shard_map/sum_partial_images/all_to_all | solution.py:201
  66.0 16.0 %copy-start = (f32[4,128]{1,0:T(4,128)S(1)}, f32[4,128]{1,0:T(4,128)}, u32[]{:S(2)}) copy-start(f32[4,128]{1,0:T(4,128)} %res_ref.3) | copy-start | bytes 6148
  66.0 16.0 %copy-start.1 = (f32[4,128]{1,0:T(4,128)S(1)}, f32[4,128]{1,0:T(4,128)}, u32[]{:S(2)}) copy-start(f32[4,128]{1,0:T(4,128)} %dir_ref.3) | copy-start | bytes 6148
  66.0 16.0 %copy-start.2 = (f32[4,128]{1,0:T(4,128)S(1)}, f32[4,128]{1,0:T(4,128)}, u32[]{:S(2)}) copy-start(f32[4,128]{1,0:T(4,128)} %sol_ref.1) | copy-start | bytes 6148

commit v7 on v6

--- a/solution.py
+++ b/solution.py
@@ -185,7 +185,7 @@
 
 
 AXIS = "d"
-YS, XS, ZS, CS = (2, 3, 0, 1), (2, 3, 0, 1), tuple((8 + k) % 16 for k in range(16)), (0, 1)
+YS, XS, ZS, CS = (2, 3, 0, 1), (2, 3, 0, 1), tuple((9 + k) % 16 for k in range(16)), (0, 1)
 
 
 def flat(y, x, z, c):

time: 83.3 us -> 83.2 us (level)
  no operation moved by 1% of the time
where the time goes in v7:
time: 83.2 us; the launch traced here: 82.8 us
  blocking collectives  39.7 us (48%)
  starting transfers between devices  18.9 us (23%)
  Pallas kernels  17.1 us (21%)
  waiting for transfers between devices  5.05 us (6%)
  between operations  1.97 us (2%)
    all_to_all x2, blocking collectives, share(): return lax.all_to_all(x, AXIS, 0, 0, axis_index_groups=groups)  39.7 us
    all_to_all x2, starting transfers between devices, share(): return lax.all_to_all(x, AXIS, 0, 0, axis_index_groups=groups)  15.3 us
    pallas_call x1, Pallas kernels, on_device(): call(product_kernel, [pltpu.VMEM((16, 16, 4, BLK), f32)], 'vvv', [((FEAT,...  14.3 us
    all_to_all x2, waiting for transfers between devices, share(): return lax.all_to_all(x, AXIS, 0, 0, axis_index_groups=groups)  4.13 us
    ppermute x1, starting transfers between devices, on_device(): t_other = lax.ppermute(t_own, AXIS, [(i, i ^ 1) for i in range(512)])  3.53 us
  transfers between devices with their start and end apart: 3, of which 2 were waited for; matrix products, arithmetic and copies ran while one was open for 0% of the time, Pallas kernels for 0%

profile of v7, /device:TPU:1, one launch (start us, length us, event | category | flops | bytes accessed | tf_op | source)
XLA Modules:
  0.0 82.8 jit_solution(17730404635262372696)
XLA Ops:
  0.6 1.5 %shard_map.94 = (f32[16,16,128]{2,1,0:T(8,128)}, f32[16,3,4,128]{3,2,1,0:T(4,128)S(1)}) custom-call(f32[1,8]{1,0:T(1,128)} %bitcast.2, f32[8,128]{1,0:T(8,128)} %pts_ref.1, f32[4,128]{1,0:T(4,128)} %res_ref.3, f32[4,128]{1,0:T(4,128)} %dir_ref.3), custom_call_target="tpu_custom_call" | custom-call | tf_op jit(solution)/shard_map/pallas_call | solution.py:209
  2.1 23.9 %all_to_all.20.own_ref = f32[16,3,4,128]{3,2,1,0:T(4,128)S(1)} all-to-all(f32[16,3,4,128]{3,2,1,0:T(4,128)S(1)} %get-tuple-element.9), channel_id=1, replica_groups={{338,340,342,344,346,348,350,320,322,324,326,328,330,332,334,336},{339,..., dimensions={0} | all-to-all | bytes 196608 | tf_op jit(solution)/shard_map/gather_in_points/all_to_all | solution.py:201
  26.0 8.7 %all-to-all-start.1 = ((f32[16,16,128]{2,1,0:T(8,128)}), f32[16,16,128]{2,1,0:T(8,128)S(1)}, u32[]{:S(2)}, u32[]{:S(2)}) async-start(f32[16,16,128]{2,1,0:T(8,128)} %get-tuple-element.12), calls=%async_computation.1 | async-start | bytes 262144 | tf_op jit(solution)/shard_map/gather_out_points/all_to_all | solution.py:201
  34.7 3.5 %collective-permute-start = (f32[16,3,4,128]{3,2,1,0:T(4,128)S(1)}, f32[16,3,4,128]{3,2,1,0:T(4,128)S(1)}, u32[]{:S(2)}, u32[]{:S(2)}) collective-permute-start(f32[16,3,4,128]{3,2,1,0:T(4,128)S(1)} %all_to_all.20.own_ref), channel_id=1, source_target_pairs={{0,1},{1,0},{2,3},{3,2},{4,5},{5,4},{6,7},{7,6},{8,9},{9,8},{10,11... | collective-permute-start | bytes 294920 | tf_op jit(solution)/shard_map/gather_in_points/ppermute | solution.py:218
  38.3 0.9 %collective-permute-done.other_ref = f32[16,3,4,128]{3,2,1,0:T(4,128)S(1)} collective-permute-done((f32[16,3,4,128]{3,2,1,0:T(4,128)S(1)}, f32[16,3,4,128]{3,2,1,0:T(4,128)S(1)}, u32[]{:S(2)}, u32[]{:S(2)}) %collective-permute-start) | collective-permute-done | bytes 98336 | tf_op jit(solution)/shard_map/gather_in_points/ppermute | solution.py:218
  39.2 0.4 shard_map.95
  39.6 0.0 all-to-all-done.1.s_ref
  39.6 14.3 %shard_map.96 = f32[16,16,4,128]{3,2,1,0:T(4,128)} custom-call(bf16[4096,64]{1,0:T(8,128)(2,1)S(1)} %get-tuple-element.10.f_ref, bf16[16,4096]{1,0:T(8,128)(2,1)S(1)} %get-tuple-element.11.d_ref, f32[16,16,128]{2,1,0:T(8,128)S(1)} %all-to-all-done.1.s_ref), custom_call_target="tpu_custom_call" | custom-call | flops 1610612736 | tf_op jit(solution)/shard_map/pallas_call | solution.py:225
  53.9 6.7 %all-to-all-start.2 = ((f32[16,16,4,128]{3,2,1,0:T(4,128)}), f32[16,16,4,128]{3,2,1,0:T(4,128)S(1)}, u32[]{:S(2)}, u32[]{:S(2)}) async-start(f32[16,16,4,128]{3,2,1,0:T(4,128)} %shard_map.96), calls=%async_computation.2 | async-start | bytes 1048576 | tf_op jit(solution)/shard_map/sum_partial_images/all_to_all | solution.py:201
  61.9 4.1 %all-to-all-done.2.parts_ref = f32[16,16,4,128]{3,2,1,0:T(4,128)S(1)} async-done(((f32[16,16,4,128]{3,2,1,0:T(4,128)}), f32[16,16,4,128]{3,2,1,0:T(4,128)S(1)}, u32[]{:S(2)}, u32[]{:S(2)}) %all-to-all-start.2) | async-done | bytes 524320 | tf_op jit(solution)/shard_map/sum_partial_images/all_to_all | solution.py:201
  66.0 0.0 copy-start
  66.0 0.0 copy-start.1
  66.0 0.0 copy-start.2
  66.0 0.2 shard_map.97
  66.2 15.8 %all_to_all.21.sums_ref = f32[32,1,128]{2,1,0:T(1,128)S(1)} all-to-all(f32[32,1,128]{2,1,0:T(1,128)S(1)} %get-tuple-element.13), channel_id=1, replica_groups={{338,339,340,341,342,343,344,345,346,347,348,349,350,351,320,321,322,32..., dimensions={0} | all-to-all | bytes 32768 | tf_op jit(solution)/shard_map/sum_scalars/all_to_all | solution.py:201
  82.0 0.0 copy-done
  82.0 0.0 copy-done.1
  82.0 0.0 copy-done.2
  82.0 0.8 shard_map.98
Async XLA Ops:
  26.0 13.5 %all-to-all-start.1 = ((f32[16,16,128]{2,1,0:T(8,128)}), f32[16,16,128]{2,1,0:T(8,128)S(1)}, u32[]{:S(2)}, u32[]{:S(2)}) async-start(f32[16,16,128]{2,1,0:T(8,128)} %get-tuple-element.12), calls=%async_computation.1 | async-start | bytes 262144 | tf_op jit(solution)/shard_map/gather_out_points/all_to_all | solution.py:201
  34.7 4.5 %collective-permute-start = (f32[16,3,4,128]{3,2,1,0:T(4,128)S(1)}, f32[16,3,4,128]{3,2,1,0:T(4,128)S(1)}, u32[]{:S(2)}, u32[]{:S(2)}) collective-permute-start(f32[16,3,4,128]{3,2,1,0:T(4,128)S(1)} %all_to_all.20.own_ref), channel_id=1, source_target_pairs={{0,1},{1,0},{2,3},{3,2},{4,5},{5,4},{6,7},{7,6},{8,9},{9,8},{10,11... | collective-permute-start | bytes 294920 | tf_op jit(solution)/shard_map/gather_in_points/ppermute | solution.py:218
  53.9 12.1 %all-to-all-start.2 = ((f32[16,16,4,128]{3,2,1,0:T(4,128)}), f32[16,16,4,128]{3,2,1,0:T(4,128)S(1)}, u32[]{:S(2)}, u32[]{:S(2)}) async-start(f32[16,16,4,128]{3,2,1,0:T(4,128)} %shard_map.96), calls=%async_computation.2 | async-start | bytes 1048576 | tf_op jit(solution)/shard_map/sum_partial_images/all_to_all | solution.py:201
  66.0 16.0 %copy-start = (f32[4,128]{1,0:T(4,128)S(1)}, f32[4,128]{1,0:T(4,128)}, u32[]{:S(2)}) copy-start(f32[4,128]{1,0:T(4,128)} %res_ref.3) | copy-start | bytes 6148
  66.0 16.0 %copy-start.1 = (f32[4,128]{1,0:T(4,128)S(1)}, f32[4,128]{1,0:T(4,128)}, u32[]{:S(2)}) copy-start(f32[4,128]{1,0:T(4,128)} %dir_ref.3) | copy-start | bytes 6148
  66.0 16.0 %copy-start.2 = (f32[4,128]{1,0:T(4,128)S(1)}, f32[4,128]{1,0:T(4,128)}, u32[]{:S(2)}) copy-start(f32[4,128]{1,0:T(4,128)} %sol_ref.1) | copy-start | bytes 6148
